TPU v7x, 32 devices: a whole 2x2x4 slice. The times are simulated.
32 devices in a mesh: orb: 16 (over z, y, core), slab: 2 (over x).
Axes of the slice: x: 2, y: 2, z: 4, core: 2. Of those that a mesh axis runs over, the one named last changes fastest.
Arguments:
- orbitals: bfloat16 [16, 64, 4096], P('orb', 'slab'), may hold values from -6 to 6
- partners: int32 [16, 2], P('orb'), may hold values from 0 to 15, as said below
- offsets: int32 [16, 3], P('orb'), may hold values from 0 to 32
- kernel: float32 [128, 128, 128], P(None, 'slab'), may hold values from 0.5 to 8
Outputs:
- exchange: float32 [16, 64, 4096], P('orb', 'slab')
Inputs may be any that keep to these rules, and one draw needn't show every extreme that they name: Orbital i's two partners differ from each other and equal (i + e) mod 16 with 1 <= e <= 4.
All inputs are finite; a program needn't handle non-finite values.
Results may differ from a plain program's by a relative error of at most 0.0042.
Values may be sent and summed in bfloat16 or wider, within the bound.
A program may use at most 128 MiB of HBM per device.

v0:
```python
from functools import partial
import math

import jax
import jax.numpy as jnp
from jax import lax
from jax.sharding import PartitionSpec as P

REACH = 4


def passed_along(block, axis, distance):
    devices = range(lax.axis_size(axis))
    route = [((i - distance) % len(devices), i) for i in devices]
    return lax.ppermute(block, axis, route)


def phase_table(length, offset, grid_len, signed):
    frequency = jnp.arange(grid_len, dtype=jnp.int32)
    places = offset + jnp.arange(length, dtype=jnp.int32)
    wrapped = places[:, None] * frequency[None, :] % grid_len
    angles = wrapped.astype(jnp.float32) * (2.0 * math.pi / grid_len)
    return (jnp.cos(angles).astype(jnp.bfloat16), (signed * jnp.sin(angles)).astype(jnp.bfloat16))


def move_box(orbital_box, displacement, row_start, row_count):
    box_edge = orbital_box.shape[1]
    rows = row_start + displacement[0] + jnp.arange(row_count, dtype=jnp.int32)
    cols = displacement[1] + jnp.arange(box_edge, dtype=jnp.int32)
    depth = displacement[2] + jnp.arange(box_edge, dtype=jnp.int32)
    picked = jnp.take(orbital_box, jnp.clip(rows, 0, box_edge - 1), axis=0)
    picked = jnp.take(picked, jnp.clip(cols, 0, box_edge - 1), axis=1)
    picked = jnp.take(picked, jnp.clip(depth, 0, box_edge - 1), axis=2)
    row_ok = (rows >= 0) & (rows < box_edge)
    col_ok = (cols >= 0) & (cols < box_edge)
    dep_ok = (depth >= 0) & (depth < box_edge)
    inside = row_ok[:, None, None] & col_ok[None, :, None] & dep_ok[None, None, :]
    return jnp.where(inside, picked, jnp.zeros_like(picked))


def product(form, left_side, right_side):
    return jnp.einsum(form, left_side, right_side, preferred_element_type=jnp.float32)


def complex_pair(form, cos_table, sin_table, real_part, imag_part):
    real_out = product(form, cos_table, real_part) - product(form, sin_table, imag_part)
    imag_out = product(form, cos_table, imag_part) + product(form, sin_table, real_part)
    return (real_out, imag_out)


def box_tables(box_edge, half_edge, grid_len, displace_part):
    own_cos, own_sin = phase_table(box_edge, half_edge, grid_len, 1.0)
    far_cos, far_sin = jax.vmap(
        lambda value: phase_table(box_edge, half_edge + value, grid_len, 1.0)
    )(displace_part)
    cos_stack = jnp.stack([jnp.broadcast_to(own_cos, far_cos.shape), far_cos], 1)
    sin_stack = jnp.stack([jnp.broadcast_to(own_sin, far_sin.shape), far_sin], 1)
    return (cos_stack, sin_stack)


def per_device(orbitals, partners, offsets, kernel):
    orb_dev = orbitals.shape[0]
    slab_rows = orbitals.shape[1]
    box_edge = math.isqrt(orbitals.shape[2])
    grid_len = 2 * box_edge
    half_edge = box_edge // 2
    spread = lax.axis_size("orb")
    slab_count = lax.axis_size("slab")
    orbit_count = orb_dev * spread
    orbit_index = lax.axis_index("orb")
    first_orbit = orbit_index * orb_dev
    slab_index = lax.axis_index("slab")
    corner_list = [offsets]
    own_full = lax.all_gather(orbitals, "slab", axis=1, tiled=True)
    box_list = [own_full]
    for hop_count in range(1, REACH + 1):
        far_box, far_corner = passed_along((own_full, offsets), "orb", -hop_count)
        box_list.append(far_box)
        corner_list.append(far_corner)
    candidates = jnp.concatenate(box_list, 0)
    corners = jnp.concatenate(corner_list, 0)
    candidates = candidates.reshape(candidates.shape[0], box_edge, box_edge, box_edge)
    pair_count = 2 * orb_dev
    partner_ids = partners.reshape(pair_count)
    owner_slot = jnp.arange(pair_count, dtype=jnp.int32) // 2
    local_slot = (partner_ids - first_orbit) % orbit_count
    displace = corners[local_slot] - offsets[owner_slot]
    fwd_cos, fwd_sin = phase_table(box_edge, half_edge, grid_len, -1.0)
    rounds = -(-pair_count // slab_count)
    picked = jnp.minimum(
        jnp.arange(rounds, dtype=jnp.int32) * slab_count + slab_index, pair_count - 1
    )
    partner_full = candidates[local_slot[picked]]
    own_boxes = candidates[owner_slot[picked]]
    shift_sel = displace[picked]
    whole_mover = jax.vmap(partial(move_box, row_count=box_edge), in_axes=(0, 0, None))
    partner_here = whole_mover(partner_full, -shift_sel, 0)
    own_there = whole_mover(own_boxes, shift_sel, 0)
    density = (own_boxes.astype(jnp.float32) * partner_here.astype(jnp.float32)).astype(
        jnp.bfloat16
    )
    z_real = product("payz,zk->payk", density, fwd_cos).astype(jnp.bfloat16)
    z_imag = product("payz,zk->payk", density, fwd_sin).astype(jnp.bfloat16)
    y_real, y_imag = complex_pair("yk,payq->pakq", fwd_cos, fwd_sin, z_real, z_imag)
    y_real, y_imag = (y_real.astype(jnp.bfloat16), y_imag.astype(jnp.bfloat16))
    kernel_full = lax.all_gather(kernel, "slab", axis=1, tiled=True)
    x_real, x_imag = complex_pair("ak,paqz->pkqz", fwd_cos, fwd_sin, y_real, y_imag)
    w_real = (kernel_full * x_real).astype(jnp.bfloat16)
    w_imag = (kernel_full * x_imag).astype(jnp.bfloat16)
    row_cos, row_sin = box_tables(box_edge, half_edge, grid_len, shift_sel[:, 0])
    v_real, v_imag = complex_pair("pmak,pkqz->pmaqz", row_cos, row_sin, w_real, w_imag)
    v_real, v_imag = (v_real.astype(jnp.bfloat16), v_imag.astype(jnp.bfloat16))
    col_cos, col_sin = box_tables(box_edge, half_edge, grid_len, shift_sel[:, 1])
    u_real, u_imag = complex_pair("pmyk,pmakz->pmayz", col_cos, col_sin, v_real, v_imag)
    u_real, u_imag = (u_real.astype(jnp.bfloat16), u_imag.astype(jnp.bfloat16))
    dep_cos, dep_sin = box_tables(box_edge, half_edge, grid_len, shift_sel[:, 2])
    field = (
        product("pmzk,pmayk->pmayz", dep_cos, u_real)
        - product("pmzk,pmayk->pmayz", dep_sin, u_imag)
    ) * (1.0 / grid_len**3)
    both_terms = jnp.stack(
        [
            field[:, 0] * partner_here.astype(jnp.float32),
            field[:, 1] * own_there.astype(jnp.float32),
        ],
        1,
    )
    arrived = lax.all_to_all(both_terms, "slab", split_axis=2, concat_axis=0, tiled=True)
    arrived = arrived.reshape(slab_count, rounds, 2, slab_rows, box_edge, box_edge)
    arrived = jnp.transpose(arrived, (1, 0, 2, 3, 4, 5)).reshape(
        rounds * slab_count, 2, slab_rows, box_edge, box_edge
    )
    arrived = arrived[:pair_count]
    own_term = arrived[:, 0]
    far_term = arrived[:, 1]
    result = own_term.reshape(orb_dev, 2, slab_rows, box_edge, box_edge).sum(1)
    hop_of_pair = (partner_ids // orb_dev - orbit_index) % spread
    slot_match = (partner_ids % orb_dev)[:, None] == jnp.arange(orb_dev, dtype=jnp.int32)[None, :]
    for hop_count in range(REACH + 1):
        weights = (slot_match & (hop_of_pair == hop_count)[:, None]).astype(jnp.float32)
        bucket = jnp.einsum("po,prst->orst", weights, far_term, precision=lax.Precision.HIGHEST)
        if hop_count == 0:
            result = result + bucket
        else:
            result = result + passed_along(bucket, "orb", hop_count)
    return result.reshape(orb_dev, slab_rows, box_edge * box_edge)


def solution(mesh):
    return jax.shard_map(
        per_device,
        mesh=mesh,
        in_specs=(P("orb", "slab", None), P("orb", None), P("orb", None), P(None, "slab", None)),
        out_specs=P("orb", "slab", None),
        check_vma=False,
    )
```

profile of v0, /device:TPU:0, one launch (start us, length us, event | category | flops | bytes accessed | tf_op | source)
XLA Modules:
  0.0 365.2 jit_solution(15364665726104492442)
XLA Ops:
  6.5 5.0 %collective-permute-start.3 = (s32[1,3]{1,0:T(1,128)}, s32[1,3]{1,0:T(1,128)S(1)}, u32[]{:S(2)}, u32[]{:S(2)}) collective-permute-start(s32[1,3]{1,0:T(1,128)} %param.12), channel_id=1, source_target_pairs={{8,0},{10,2},{12,4},{14,6},{16,8},{18,10},{20,12},{22,14},{24,16},... | collective-permute-start | bytes 44 | tf_op jit(solution)/shard_map/ppermute | solution.py:15
  14.3 8.3 %all_gather.7 = bf16[1,64,4096]{2,1,0:T(8,128)(2,1)S(1)} all-gather(bf16[1,32,4096]{2,1,0:T(8,128)(2,1)} %param.10), channel_id=1, replica_groups=mesh['orb'=16,'slab'=2] {'slab'}, dimensions={1}, use_global_device_ids=true | all-gather | bytes 786432 | tf_op jit(solution)/shard_map/all_gather | solution.py:74
  23.1 6.6 %copy.37 = f32[128,64,128]{2,0,1:T(8,128)} copy(f32[128,64,128]{2,1,0:T(8,128)} %param.13) | data formatting | bytes 8388608 | tf_op args[3]
  35.7 2.8 collective-permute-start.5
  38.5 2.7 collective-permute-start.4
  57.2 7.6 %collective-permute-done.4 = bf16[1,64,4096]{2,1,0:T(8,128)(2,1)} collective-permute-done((bf16[1,64,4096]{2,1,0:T(8,128)(2,1)S(1)}, bf16[1,64,4096]{2,1,0:T(8,128)(2,1)}, u32[]{:S(2)}, u32[]{:S(2)}) %collective-permute-start.4) | collective-permute-done | bytes 524320 | tf_op jit(solution)/shard_map/ppermute | solution.py:15
  69.2 6.7 %reshape.1068 = bf16[5,64,64,64]{3,2,1,0:T(8,128)(2,1)} reshape(bf16[5,64,4096]{2,1,0:T(8,128)(2,1)S(1)} %constant_dynamic-update-slice_fusion) | data formatting | bytes 5242880 | tf_op jit(solution)/shard_map/reshape | solution.py:82
  75.9 1.7 constant_dynamic-slice_fusion
  80.1 2.2 copy.40
  82.3 1.7 gather_fusion.3
  84.1 2.2 copy.41
  87.2 1.7 copy.54
  88.9 2.0 gather_fusion.5
  92.1 3.3 copy.55
  97.0 2.9 copy.56
  103.5 2.3 fusion.29
  105.8 3.7 %copy.42 = bf16[64,128,128]{2,0,1:T(8,128)(2,1)S(1)} copy(bf16[64,128,128]{1,2,0:T(8,128)(2,1)} %fusion.29) | data formatting | bytes 4194304 | tf_op jit(solution)/shard_map/reshape.27
  109.5 2.2 fusion.108
  111.7 2.2 fusion.30
  113.9 4.2 %copy.43 = bf16[64,128,128]{2,0,1:T(8,128)(2,1)} copy(bf16[64,128,128]{1,2,0:T(8,128)(2,1)} %fusion.30) | data formatting | bytes 4194304 | tf_op jit(solution)/shard_map/reshape.33
  118.1 6.3 %fusion.106 = f32[128,128,128]{2,1,0:T(8,128)} fusion(bf16[64,128,128]{2,0,1:T(8,128)(2,1)} %copy.43, s32[64]{0:T(128)S(1)} %iota_add_fusion.3), kind=kOutput, calls=%fused_computation.142 | convolution fusion | flops 268558336 | bytes 10486016 | tf_op jit(solution)/shard_map/ak,paqz->pkqz/dot_general | solution.py:42
  124.4 4.7 %fusion.110 = f32[128,128,128]{2,1,0:T(8,128)} fusion(bf16[64,128,128]{2,0,1:T(8,128)(2,1)S(1)} %copy.42, s32[64]{0:T(128)S(1)} %iota_add_fusion.3), kind=kOutput, calls=%fused_computation.144 | convolution fusion | flops 268558336 | bytes 10486016 | tf_op jit(solution)/shard_map/ak,paqz->pkqz/dot_general | solution.py:42
  129.1 4.8 %all-gather.2.cloned.1.call-done = f32[128,128,128]{2,0,1:T(8,128)} async-done(((f32[128,64,128]{2,0,1:T(8,128)}), f32[128,128,128]{2,0,1:T(8,128)}) %all-gather.2.cloned.1.call-update) | async-done | bytes 8388624 | tf_op jit(solution)/shard_map/all_gather | solution.py:106
  133.9 9.0 %copy.38 = f32[128,128,128]{0,2,1:T(8,128)} copy(f32[128,128,128]{2,0,1:T(8,128)} %all-gather.2.cloned.1.call-done) | data formatting | bytes 16777216 | tf_op jit(solution)/shard_map/all_gather | solution.py:106
  142.9 7.4 %fusion.3 = bf16[128,128,128,1]{0,2,1,3:T(8,128)(2,1)S(1)} fusion(f32[128,128,128]{2,1,0:T(8,128)} %fusion.106, f32[128,128,128]{0,2,1:T(8,128)} %copy.38, bf16[64,128,128]{2,0,1:T(8,128)(2,1)S(1)} %copy.42, s32[64]{0:T(128)S(1)} %iota_add_fusion.3), kind=kOutput, calls=%fused_computation.14 | convolution fusion | flops 274857984 | bytes 23068928 | tf_op jit(solution)/shard_map/ak,paqz->pkqz/dot_general | solution.py:42
  151.7 5.1 %fusion.2 = bf16[128,128,128,1]{0,2,1,3:T(8,128)(2,1)S(1)} fusion(f32[128,128,128]{2,1,0:T(8,128)} %fusion.110, f32[128,128,128]{0,2,1:T(8,128)S(1)} %copy-done, bf16[64,128,128]{2,0,1:T(8,128)(2,1)S(1)} %copy-done.1, s32[64]{0:T(128)S(1)} %iota_add_fusion.3), kind=kOutput, calls=%fused_computation.13 | convolution fusion | flops 274857984 | bytes 23068928 | tf_op jit(solution)/shard_map/ak,paqz->pkqz/dot_general | solution.py:42
  156.8 4.5 %fusion.95 = f32[2,64,128,128]{3,1,2,0:T(8,128)} fusion(bf16[128,128,128,1]{0,2,1,3:T(8,128)(2,1)S(1)} %fusion.2, bf16[1,1,64,128]{3,2,1,0:T(8,128)(2,1)S(1)} %get-tuple-element.105, bf16[1,1,64,128]{3,2,1,0:T(8,128)(2,1)S(1)} %get-tuple-element.79), kind=kOutput, calls=%fused_computation.139 | convolution fusion | flops 536936448 | bytes 12615680 | tf_op jit(solution)/shard_map/pmak,pkqz->pmaqz/dot_general | solution.py:42
  162.6 6.8 %subtract_convert_fusion = bf16[2,64,128,128]{3,1,2,0:T(8,128)(2,1)} fusion(f32[2,64,128,128]{3,1,2,0:T(8,128)} %fusion.95, bf16[128,128,128,1]{0,2,1,3:T(8,128)(2,1)S(1)} %fusion.3, bf16[1,1,64,128]{3,2,1,0:T(8,128)(2,1)S(1)} %get-tuple-element.106, bf16[1,1,64,128]{3,2,1,0:T(8,128)(2,1)S(1)} %get-tuple-element.78), kind=kOutput, calls=%fused_computation.12 | convolution fusion | flops 541130752 | bytes 16809984 | tf_op jit(solution)/shard_map/pmak,pkqz->pmaqz/dot_general | solution.py:42
  170.6 4.8 %fusion.4 = f32[2,64,128,64]{2,3,1,0:T(8,128)} fusion(bf16[2,64,128,128]{3,1,2,0:T(8,128)(2,1)S(1)} %add_convert_fusion, bf16[1,1,64,128]{3,2,1,0:T(8,128)(2,1)S(1)} %get-tuple-element.106, bf16[1,1,64,128]{3,2,1,0:T(8,128)(2,1)S(1)} %get-tuple-element.107), kind=kOutput, calls=%fused_computation.21 | convolution fusion | flops 268500992 | bytes 8421376 | tf_op jit(solution)/shard_map/pmyk,pmakz->pmayz/dot_general | solution.py:42
  175.5 5.0 %fusion.6 = f32[2,64,128,64]{2,3,1,0:T(8,128)} fusion(bf16[2,64,128,128]{3,1,2,0:T(8,128)(2,1)S(1)} %add_convert_fusion, bf16[1,1,64,128]{3,2,1,0:T(8,128)(2,1)S(1)} %get-tuple-element.105, bf16[1,1,64,128]{3,2,1,0:T(8,128)(2,1)S(1)} %get-tuple-element.108), kind=kOutput, calls=%fused_computation.23 | convolution fusion | flops 268500992 | bytes 8421376 | tf_op jit(solution)/shard_map/pmyk,pmakz->pmayz/dot_general | solution.py:42
  180.4 9.0 %fusion.15 = f32[2,64,64,64]{3,2,1,0:T(8,128)} fusion(f32[2,64,128,64]{2,3,1,0:T(8,128)} %fusion.4, bf16[2,64,128,128]{3,1,2,0:T(8,128)(2,1)} %subtract_convert_fusion, bf16[1,1,64,128]{3,2,1,0:T(8,128)(2,1)S(1)} %get-tuple-element.105, bf16[1,1,64,128]{3,2,1,0:T(8,128)(2,1)S(1)} %get-tuple-element.72, bf16[1,1,64,128]{3,2,1,0:T(8,128)(2,1)S(1)} %get-tuple-element.108), kind=kOutput, calls=%fused_computation.34 | convolution fusion | flops 404832256 | bytes 10534912 | tf_op jit(solution)/shard_map/pmzk,pmayk->pmayz/dot_general | solution.py:42
  189.4 10.3 %multiply_bitcast_fusion = f32[1,2,64,64,64]{4,3,2,1,0:T(8,128)} fusion(f32[2,64,64,64]{3,2,1,0:T(8,128)} %fusion.15, f32[2,64,128,64]{2,3,1,0:T(8,128)} %fusion.6, bf16[2,64,128,128]{3,1,2,0:T(8,128)(2,1)} %subtract_convert_fusion, bf16[1,1,64,128]{3,2,1,0:T(8,128)(2,1)S(1)} %get-tuple-element.106, bf16[1,1,64,128]{3,2,1,0:T(8,128)(2,1)S(1)} %get-tuple-element.71, ...), kind=kOutput, calls=%fused_computation.16 | convolution fusion | flops 405880832 | bytes 12632064 | tf_op jit(solution)/shard_map/pmzk,pmayk->pmayz/dot_general | solution.py:42
  199.7 3.5 fusion.13
  203.3 2.4 copy_bitcast_fusion
  205.7 4.2 %reshape.1299 = f32[2,1,262144]{2,1,0:T(1,128)S(1)} reshape(f32[64,1,2,64,64]{4,3,2,1,0:T(8,128)} %copy_bitcast_fusion) | data formatting | bytes 4194304
  209.9 28.7 %all_to_all.18 = f32[2,1,262144]{2,1,0:T(1,128)} all-to-all(f32[2,1,262144]{2,1,0:T(1,128)S(1)} %reshape.1299), channel_id=1, replica_groups=mesh['orb'=16,'slab'=2] {'slab'}, dimensions={0} | all-to-all | bytes 4194304 | tf_op jit(solution)/shard_map/all_to_all | solution.py:128
  239.1 8.1 %reduce.2 = f32[2,262144]{1,0:T(2,128)S(1)} reduce(f32[2,1,262144]{2,1,0:T(1,128)} %all_to_all.18, f32[]{:T(128)} %broadcast.1746), dimensions={1}, to_apply=%all_to_all.13.reduce_sub_computation | reduce | bytes 4194308 | tf_op jit(solution)/shard_map/all_to_all | solution.py:128
  247.2 4.3 %reshape.1300 = f32[64,1,2,64,64]{4,3,2,1,0:T(8,128)} reshape(f32[2,262144]{1,0:T(2,128)S(1)} %reduce.2) | data formatting | bytes 4194304
  251.5 2.7 slice_reduce_fusion
  254.2 4.7 %fusion.41 = f32[1,32,64,64]{3,0,2,1:T(1,128)S(1)} fusion(f32[2,32,64,64]{3,2,1,0:T(8,128)S(1)} %get-tuple-element.68, s32[1,2]{1,0:T(1,128)S(1)} %copy-done.7, s32[]{:T(128)S(6)} %axis_index.23), kind=kOutput, calls=%fused_computation.65 | convolution fusion | flops 3145754 | bytes 1572876 | tf_op jit(solution)/shard_map/po,prst->orst/dot_general | solution.py:141
  258.9 4.7 %fusion.39 = f32[1,32,64,64]{3,0,2,1:T(1,128)S(1)} fusion(f32[2,32,64,64]{3,2,1,0:T(8,128)S(1)} %get-tuple-element.68, s32[1,2]{1,0:T(1,128)S(1)} %copy-done.7, s32[]{:T(128)S(6)} %axis_index.23), kind=kOutput, calls=%fused_computation.63 | convolution fusion | flops 3145754 | bytes 1572876 | tf_op jit(solution)/shard_map/po,prst->orst/dot_general | solution.py:141
  263.6 4.9 %fusion.37 = f32[1,32,64,64]{3,0,2,1:T(1,128)S(1)} fusion(f32[2,32,64,64]{3,2,1,0:T(8,128)S(1)} %get-tuple-element.68, s32[1,2]{1,0:T(1,128)S(1)} %copy-done.7, s32[]{:T(128)S(6)} %axis_index.23), kind=kOutput, calls=%fused_computation.61 | convolution fusion | flops 3145754 | bytes 1572876 | tf_op jit(solution)/shard_map/po,prst->orst/dot_general | solution.py:141
  268.5 4.7 %fusion.35 = f32[1,32,64,64]{3,0,2,1:T(1,128)S(1)} fusion(f32[2,32,64,64]{3,2,1,0:T(8,128)S(1)} %get-tuple-element.68, s32[1,2]{1,0:T(1,128)S(1)} %copy-done.7, s32[]{:T(128)S(6)} %axis_index.23), kind=kOutput, calls=%fused_computation.59 | convolution fusion | flops 3145754 | bytes 1572876 | tf_op jit(solution)/shard_map/po,prst->orst/dot_general | solution.py:141
  277.6 4.7 %fusion.43 = f32[1,32,64,64]{3,0,2,1:T(1,128)S(1)} fusion(f32[2,32,64,64]{3,2,1,0:T(8,128)S(1)} %get-tuple-element.68, s32[1,2]{1,0:T(1,128)S(1)} %copy-done.7, s32[]{:T(128)S(6)} %axis_index.23), kind=kOutput, calls=%fused_computation.67 | convolution fusion | flops 3145754 | bytes 1572876 | tf_op jit(solution)/shard_map/po,prst->orst/dot_general | solution.py:141
  282.3 18.9 %collective-permute-done.11 = f32[1,32,64,64]{3,2,1,0:T(8,128)S(1)} collective-permute-done((f32[1,32,64,64]{3,2,1,0:T(8,128)S(1)}, f32[1,32,64,64]{3,2,1,0:T(8,128)S(1)}, u32[]{:S(2)}, u32[]{:S(2)}) %collective-permute-start.11) | collective-permute-done | bytes 524320 | tf_op jit(solution)/shard_map/ppermute | solution.py:15
  301.2 9.2 %collective-permute-done.10 = f32[1,32,64,64]{3,2,1,0:T(8,128)S(1)} collective-permute-done((f32[1,32,64,64]{3,2,1,0:T(8,128)S(1)}, f32[1,32,64,64]{3,2,1,0:T(8,128)S(1)}, u32[]{:S(2)}, u32[]{:S(2)}) %collective-permute-start.10) | collective-permute-done | bytes 524320 | tf_op jit(solution)/shard_map/ppermute | solution.py:15
  310.4 36.7 %collective-permute-done.9 = f32[1,32,64,64]{3,2,1,0:T(8,128)S(1)} collective-permute-done((f32[1,32,64,64]{3,2,1,0:T(8,128)S(1)}, f32[1,32,64,64]{3,2,1,0:T(8,128)S(1)}, u32[]{:S(2)}, u32[]{:S(2)}) %collective-permute-start.9) | collective-permute-done | bytes 524320 | tf_op jit(solution)/shard_map/ppermute | solution.py:15
  347.1 9.2 %collective-permute-done.8 = f32[1,32,64,64]{3,2,1,0:T(8,128)S(1)} collective-permute-done((f32[1,32,64,64]{3,2,1,0:T(8,128)S(1)}, f32[1,32,64,64]{3,2,1,0:T(8,128)S(1)}, u32[]{:S(2)}, u32[]{:S(2)}) %collective-permute-start.8) | collective-permute-done | bytes 524320 | tf_op jit(solution)/shard_map/ppermute | solution.py:15
  (96 shorter events, 44.2 us)
Async XLA Ops:
  6.5 127.4 %all-gather.2.cloned.1.call-start = ((), (), s32[]{:S(2)}) async-start(), calls=%async_computation.1 | async-start | bytes 12582912 | tf_op jit(solution)/shard_map/all_gather | solution.py:106
  6.5 28.7 %collective-permute-start.3 = (s32[1,3]{1,0:T(1,128)}, s32[1,3]{1,0:T(1,128)S(1)}, u32[]{:S(2)}, u32[]{:S(2)}) collective-permute-start(s32[1,3]{1,0:T(1,128)} %param.12), channel_id=1, source_target_pairs={{8,0},{10,2},{12,4},{14,6},{16,8},{18,10},{20,12},{22,14},{24,16},... | collective-permute-start | bytes 44 | tf_op jit(solution)/shard_map/ppermute | solution.py:15
  11.6 24.1 %collective-permute-start.2 = (s32[1,3]{1,0:T(1,128)}, s32[1,3]{1,0:T(1,128)S(1)}, u32[]{:S(2)}, u32[]{:S(2)}) collective-permute-start(s32[1,3]{1,0:T(1,128)} %param.12), channel_id=1, source_target_pairs={{6,0},{8,2},{10,4},{12,6},{14,8},{16,10},{18,12},{20,14},{22,16},{... | collective-permute-start | bytes 44 | tf_op jit(solution)/shard_map/ppermute | solution.py:15
  11.6 26.9 %collective-permute-start.1 = (s32[1,3]{1,0:T(1,128)}, s32[1,3]{1,0:T(1,128)S(1)}, u32[]{:S(2)}, u32[]{:S(2)}) collective-permute-start(s32[1,3]{1,0:T(1,128)} %param.12), channel_id=1, source_target_pairs={{4,0},{6,2},{8,4},{10,6},{12,8},{14,10},{16,12},{18,14},{20,16},{2... | collective-permute-start | bytes 44 | tf_op jit(solution)/shard_map/ppermute | solution.py:15
  13.0 28.2 %collective-permute-start = (s32[1,3]{1,0:T(1,128)}, s32[1,3]{1,0:T(1,128)S(1)}, u32[]{:S(2)}, u32[]{:S(2)}) collective-permute-start(s32[1,3]{1,0:T(1,128)} %param.12), channel_id=1, source_target_pairs={{2,0},{4,2},{6,4},{8,6},{10,8},{12,10},{14,12},{16,14},{18,16},{20... | collective-permute-start | bytes 44 | tf_op jit(solution)/shard_map/ppermute | solution.py:15
  22.6 45.5 %collective-permute-start.7 = (bf16[1,64,4096]{2,1,0:T(8,128)(2,1)S(1)}, bf16[1,64,4096]{2,1,0:T(8,128)(2,1)}, u32[]{:S(2)}, u32[]{:S(2)}) collective-permute-start(bf16[1,64,4096]{2,1,0:T(8,128)(2,1)S(1)} %all_gather.7), channel_id=1, source_target_pairs={{8,0},{10,2},{12,4},{14,6},{16,8},{18,10},{20,12},{22,14},{24,16},... | collective-permute-start | bytes 1572872 | tf_op jit(solution)/shard_map/ppermute | solution.py:15
  29.7 0.7 copy-start.7
  29.7 11.5 %copy-start.6 = (s32[1,3]{1,0:T(1,128)S(1)}, s32[1,3]{1,0:T(1,128)}, u32[]{:S(2)}) copy-start(s32[1,3]{1,0:T(1,128)} %param.12) | copy-start | bytes 40
  35.2 31.7 %collective-permute-start.6 = (bf16[1,64,4096]{2,1,0:T(8,128)(2,1)S(1)}, bf16[1,64,4096]{2,1,0:T(8,128)(2,1)}, u32[]{:S(2)}, u32[]{:S(2)}) collective-permute-start(bf16[1,64,4096]{2,1,0:T(8,128)(2,1)S(1)} %all_gather.7), channel_id=1, source_target_pairs={{6,0},{8,2},{10,4},{12,6},{14,8},{16,10},{18,12},{20,14},{22,16},{... | collective-permute-start | bytes 1572872 | tf_op jit(solution)/shard_map/ppermute | solution.py:15
  35.7 30.2 %collective-permute-start.5 = (bf16[1,64,4096]{2,1,0:T(8,128)(2,1)S(1)}, bf16[1,64,4096]{2,1,0:T(8,128)(2,1)}, u32[]{:S(2)}, u32[]{:S(2)}) collective-permute-start(bf16[1,64,4096]{2,1,0:T(8,128)(2,1)S(1)} %all_gather.7), channel_id=1, source_target_pairs={{4,0},{6,2},{8,4},{10,6},{12,8},{14,10},{16,12},{18,14},{20,16},{2... | collective-permute-start | bytes 1572872 | tf_op jit(solution)/shard_map/ppermute | solution.py:15
  38.5 26.4 %collective-permute-start.4 = (bf16[1,64,4096]{2,1,0:T(8,128)(2,1)S(1)}, bf16[1,64,4096]{2,1,0:T(8,128)(2,1)}, u32[]{:S(2)}, u32[]{:S(2)}) collective-permute-start(bf16[1,64,4096]{2,1,0:T(8,128)(2,1)S(1)} %all_gather.7), channel_id=1, source_target_pairs={{2,0},{4,2},{6,4},{8,6},{10,8},{12,10},{14,12},{16,14},{18,16},{20... | collective-permute-start | bytes 1572872 | tf_op jit(solution)/shard_map/ppermute | solution.py:15
  101.3 2.2 copy-start.5
  102.5 1.0 copy-start.3
  109.5 2.2 copy-start.4
  142.9 8.2 %copy-start = (f32[128,128,128]{0,2,1:T(8,128)S(1)}, f32[128,128,128]{0,2,1:T(8,128)}, u32[]{:S(2)}) copy-start(f32[128,128,128]{0,2,1:T(8,128)} %copy.38) | copy-start | bytes 25165828
  142.9 8.7 %copy-start.1 = (bf16[64,128,128]{2,0,1:T(8,128)(2,1)S(1)}, bf16[64,128,128]{2,0,1:T(8,128)(2,1)}, u32[]{:S(2)}) copy-start(bf16[64,128,128]{2,0,1:T(8,128)(2,1)} %copy.43) | copy-start | bytes 6291460
  189.4 10.3 %copy-start.2 = (bf16[64,64,64]{0,2,1:T(8,128)(2,1)S(1)}, bf16[64,64,64]{0,2,1:T(8,128)(2,1)}, u32[]{:S(2)}) copy-start(bf16[64,64,64]{0,2,1:T(8,128)(2,1)} %copy.56) | copy-start | bytes 1572868
  273.2 27.9 %collective-permute-start.11 = (f32[1,32,64,64]{3,2,1,0:T(8,128)S(1)}, f32[1,32,64,64]{3,2,1,0:T(8,128)S(1)}, u32[]{:S(2)}, u32[]{:S(2)}) collective-permute-start(f32[1,32,64,64]{3,2,1,0:T(8,128)S(1)} %bitcast.320), channel_id=1, source_target_pairs={{24,0},{26,2},{28,4},{30,6},{0,8},{2,10},{4,12},{6,14},{8,16},{10,... | collective-permute-start | bytes 1572872 | tf_op jit(solution)/shard_map/ppermute | solution.py:15
  274.8 35.6 %collective-permute-start.10 = (f32[1,32,64,64]{3,2,1,0:T(8,128)S(1)}, f32[1,32,64,64]{3,2,1,0:T(8,128)S(1)}, u32[]{:S(2)}, u32[]{:S(2)}) collective-permute-start(f32[1,32,64,64]{3,2,1,0:T(8,128)S(1)} %bitcast.319), channel_id=1, source_target_pairs={{26,0},{28,2},{30,4},{0,6},{2,8},{4,10},{6,12},{8,14},{10,16},{12,... | collective-permute-start | bytes 1572872 | tf_op jit(solution)/shard_map/ppermute | solution.py:15
  274.8 72.3 %collective-permute-start.9 = (f32[1,32,64,64]{3,2,1,0:T(8,128)S(1)}, f32[1,32,64,64]{3,2,1,0:T(8,128)S(1)}, u32[]{:S(2)}, u32[]{:S(2)}) collective-permute-start(f32[1,32,64,64]{3,2,1,0:T(8,128)S(1)} %bitcast.318), channel_id=1, source_target_pairs={{28,0},{30,2},{0,4},{2,6},{4,8},{6,10},{8,12},{10,14},{12,16},{14,... | collective-permute-start | bytes 1572872 | tf_op jit(solution)/shard_map/ppermute | solution.py:15
  276.3 80.0 %collective-permute-start.8 = (f32[1,32,64,64]{3,2,1,0:T(8,128)S(1)}, f32[1,32,64,64]{3,2,1,0:T(8,128)S(1)}, u32[]{:S(2)}, u32[]{:S(2)}) collective-permute-start(f32[1,32,64,64]{3,2,1,0:T(8,128)S(1)} %bitcast.317), channel_id=1, source_target_pairs={{30,0},{0,2},{2,4},{4,6},{6,8},{8,10},{10,12},{12,14},{14,16},{16,... | collective-permute-start | bytes 1572872 | tf_op jit(solution)/shard_map/ppermute | solution.py:15
Sparse Core Ops, SparseCore 0:
  29.9 104.0 all-gather.1
where the time goes:
time: 370 us; the launch traced here: 365 us
  matrix products  100 us (27%)
  waiting for transfers between devices  86.5 us (23%)
  local copies, waits for them, and re-layouts  72.1 us (19%)
  blocking collectives  37 us (10%)
  other arithmetic  31.3 us (8%)
  between operations  19.6 us (5%)
  starting transfers between devices  18.5 us (5%)
    ppermute x12, waiting for transfers between devices, passed_along(): return lax.ppermute(block, axis, route)  81.6 us
    dot_general x18, matrix products, product(): jnp.einsum(form, left_side, right_side, preferred_element_type=jnp.float32)  76.5 us
    all_to_all x1, blocking collectives, per_device(): lax.all_to_all(both_terms, 'slab', split_axis=2, concat_axis=0, tiled=True)  28.7 us
    dot_general x5, matrix products, per_device(): jnp.einsum('po,prst->orst', weights, far_term, precision=lax.Precision.HI...  23.7 us
    unnamed x23, local copies, waits for them, and re-layouts  20.4 us
    ppermute x12, starting transfers between devices, passed_along(): return lax.ppermute(block, axis, route)  18.5 us
    all_gather x1, local copies, waits for them, and re-layouts, per_device(): kernel_full = lax.all_gather(kernel, 'slab', axis=1, tiled=True)  8.99 us
    gather x6, local copies, waits for them, and re-layouts, move_box(): picked = jnp.take(picked, jnp.clip(depth, 0, box_edge - 1), axis=2)  8.53 us
  transfers between devices with their start and end apart: 13, of which 6 were waited for; matrix products, arithmetic and copies ran while one was open for 25% of the time, Pallas kernels for 0%

commit v1 on v0

v1 whole, which is shorter than its diff:
```python
import functools
import math

import jax
import jax.numpy as jnp
import ml_dtypes
import numpy as np
from jax import lax
from jax.experimental import pallas as pl
from jax.experimental.pallas import tpu as pltpu
from jax.sharding import PartitionSpec as P

REACH = 4
F32 = jnp.float32
BF16 = jnp.bfloat16


def passed_along(block, axis, distance):
    devices = range(lax.axis_size(axis))
    route = [((i - distance) % len(devices), i) for i in devices]
    return lax.ppermute(block, axis, route)


def phases(places, frequency, grid_len, signed):
    wrapped = (places[:, None] * frequency[None, :]) % grid_len
    angles = wrapped.astype(np.float64) * (2.0 * math.pi / grid_len)
    return np.cos(angles), signed * np.sin(angles)


def block_form(cos, sin):
    return np.block([[cos, -sin], [sin, cos]])


def make_tables(box_edge, slab_count):
    grid_len = 2 * box_edge
    half = box_edge // 2
    k1_count = grid_len // slab_count
    box = np.arange(box_edge) + half
    grid = np.arange(grid_len)
    cos, sin = phases(box, grid, grid_len, -1.0)
    f2 = np.zeros((2 * box_edge, 2 * grid_len))
    f2[:box_edge] = np.concatenate([cos, sin], 1)
    f0 = block_form(cos.T, sin.T)
    f1 = []
    e1 = []
    gcos, gsin = phases(grid, grid, grid_len, 1.0)
    for s in range(slab_count):
        mine = slice(s * k1_count, (s + 1) * k1_count)
        f1.append(block_form(cos.T[mine], sin.T[mine]))
        e1.append(block_form(gcos[:, mine], gsin[:, mine]))
    e0 = block_form(gcos, gsin)
    e2 = np.concatenate([gcos.T, -gsin.T], 0) / grid_len**3
    tables = [f2, np.stack(f1), f0, e0, np.stack(e1), e2]
    return [t.astype(np.float32).astype(ml_dtypes.bfloat16) for t in tables]


def dot(a, b):
    return jnp.dot(a, b, preferred_element_type=F32)


def pair_kernel(
    box_edge, k1_count,
    shift_ref, slab_ref,
    boxes_ref, kernel_ref, f2_ref, f1_ref, f0_ref, e0_ref, e1_ref, e2_ref,
    out_ref,
    cells, here, y_parts, v_parts, terms, e1_own, e1_far, e2_own, e2_far,
):
    edge = box_edge
    grid_len = 2 * edge
    half = edge // 2
    lanes = 2 * edge
    slab = slab_ref[0]
    lane = lax.broadcasted_iota(jnp.int32, (edge, lanes), 1)
    low_lanes = lane < edge
    row = lax.broadcasted_iota(jnp.int32, (edge, lanes), 0)
    shifts = [[shift_ref[n, c] for c in range(3)] for n in range(2)]

    e1_grid = e1_ref[slab]
    e2_grid = e2_ref[...]
    sel_lane = lax.broadcasted_iota(jnp.int32, (grid_len, lanes), 1)
    sel_row = lax.broadcasted_iota(jnp.int32, (grid_len, lanes), 0)

    def windows(d1, d2):
        pick_rows = (row + half + d1 == lane).astype(F32).astype(BF16)
        top = dot(pick_rows, e1_grid[:grid_len]).astype(BF16)
        bottom = dot(pick_rows, e1_grid[grid_len:]).astype(BF16)
        pick_cols = ((sel_lane + half + d2 == sel_row) & (sel_lane < edge)).astype(F32).astype(BF16)
        return jnp.concatenate([top, bottom], 0), dot(e2_grid, pick_cols).astype(BF16)

    e1_own[...], e2_own[...] = windows(0, 0)
    for n in range(2):
        e1_far[n], e2_far[n] = windows(shifts[n][1], shifts[n][2])

    def unpack(g, carry):
        lo_at = pl.ds(2 * g, edge, stride=edge)
        hi_at = pl.ds(2 * g + 1, edge, stride=edge)
        for b in range(3):
            both = boxes_ref[b, :, pl.ds(pl.multiple_of(g * lanes, lanes), lanes)].astype(F32)
            cells[b, lo_at, :] = jnp.where(low_lanes, both, 0.0)
            cells[b, hi_at, :] = jnp.where(low_lanes, pltpu.roll(both, edge, 1), 0.0)
        return carry

    lax.fori_loop(0, edge // 2, unpack, 0, unroll=2)

    def moved(b, c0, d0, d1, d2):
        source = c0 + d0
        at = jnp.clip(source, 0, edge - 1)
        block = cells[b, pl.ds(pl.multiple_of(at * edge, edge), edge), :]
        block = pltpu.roll(block, (-d2) & (lanes - 1), 1)
        block = pltpu.roll(block, (-d1) & (edge - 1), 0)
        inside = (row + d1 >= 0) & (row + d1 < edge) & (source >= 0) & (source < edge)
        return jnp.where(inside, block, 0.0)

    def forward(c0, carry):
        at = pl.ds(pl.multiple_of(c0 * edge, edge), edge)
        own = cells[0, at, :]
        z = []
        for n in range(2):
            d0, d1, d2 = shifts[n]
            partner = moved(1 + n, c0, -d0, -d1, -d2)
            here[n, at, :] = partner
            z.append((own * partner).astype(BF16))
        z = dot(jnp.concatenate(z, 0), f2_ref[...]).astype(BF16)
        z = jnp.concatenate(
            [
                jnp.concatenate([z[n * edge : (n + 1) * edge, :grid_len], z[n * edge : (n + 1) * edge, grid_len:]], 0)
                for n in range(2)
            ],
            1,
        )
        y = dot(f1_ref[slab], z)
        for n in range(2):
            part = y[:, n * grid_len : (n + 1) * grid_len]
            y_parts[n, pl.ds(c0, k1_count, stride=2 * edge), :] = part[:k1_count]
            y_parts[n, pl.ds(edge + c0, k1_count, stride=2 * edge), :] = part[k1_count:]
        return carry

    lax.fori_loop(0, edge, forward, 0, unroll=4)

    def middle(k1, carry):
        at = pl.ds(pl.multiple_of(k1 * 2 * edge, 2 * edge), 2 * edge)
        y = jnp.concatenate([y_parts[n, at, :].astype(BF16) for n in range(2)], 1)
        x = dot(f0_ref[...], y)
        k = kernel_ref[pl.ds(k1, grid_len, stride=k1_count), :]
        k = jnp.concatenate([k, k], 1)
        w = jnp.concatenate([(x[:grid_len] * k).astype(BF16), (x[grid_len:] * k).astype(BF16)], 0)
        v = dot(e0_ref[...], w)
        for n in range(2):
            part = v[:, n * grid_len : (n + 1) * grid_len]
            v_parts[n, pl.ds(k1, grid_len, stride=2 * k1_count), :] = part[:grid_len]
            v_parts[n, pl.ds(k1_count + k1, grid_len, stride=2 * k1_count), :] = part[grid_len:]
        return carry

    lax.fori_loop(0, k1_count, middle, 0, unroll=4)

    def v_rows(n, u0):
        at = pl.ds(pl.multiple_of(u0 * 2 * k1_count, 2 * k1_count), 2 * k1_count)
        return v_parts[n, at, :].astype(BF16)

    def backward(c0, carry):
        at = pl.ds(pl.multiple_of(c0 * edge, edge), edge)
        v = jnp.concatenate([v_rows(n, half + c0) for n in range(2)], 1)
        u = dot(e1_own[...], v).astype(BF16)
        u = jnp.concatenate(
            [
                jnp.concatenate([u[:edge, n * grid_len : (n + 1) * grid_len], u[edge:, n * grid_len : (n + 1) * grid_len]], 1)
                for n in range(2)
            ],
            0,
        )
        field = dot(u, e2_own[...])
        terms[0, at, :] = field[:edge] * here[0, at, :] + field[edge:] * here[1, at, :]
        for n in range(2):
            d0, d1, d2 = shifts[n]
            u = dot(e1_far[n], v_rows(n, half + d0 + c0)).astype(BF16)
            field = dot(jnp.concatenate([u[:edge], u[edge:]], 1), e2_far[n])
            terms[1 + n, at, :] = field * moved(0, c0, d0, d1, d2)
        return carry

    lax.fori_loop(0, edge, backward, 0, unroll=4)

    def pack(g, carry):
        for b in range(3):
            lo = terms[b, pl.ds(2 * g, edge, stride=edge), :]
            hi = terms[b, pl.ds(2 * g + 1, edge, stride=edge), :]
            both = lo + pltpu.roll(hi, edge, 1)
            out_ref[b, :, pl.ds(pl.multiple_of(g * lanes, lanes), lanes)] = both.astype(BF16)
        return carry

    lax.fori_loop(0, edge // 2, pack, 0, unroll=2)


def pair_terms(boxes, displace, slab_index, kernel, slab_count):
    box_edge = boxes.shape[1]
    grid_len, k1_count = kernel.shape[0], kernel.shape[1]
    tables = make_tables(box_edge, slab_count)
    smem = pl.BlockSpec(memory_space=pltpu.SMEM)
    vmem = pl.BlockSpec(memory_space=pltpu.VMEM)
    cells = box_edge * box_edge
    lanes = 2 * box_edge
    return pl.pallas_call(
        functools.partial(pair_kernel, box_edge, k1_count),
        out_shape=jax.ShapeDtypeStruct(boxes.shape, BF16),
        in_specs=[smem, smem] + [vmem] * 8,
        out_specs=vmem,
        scratch_shapes=[
            pltpu.VMEM((3, cells, lanes), F32),
            pltpu.VMEM((2, cells, lanes), F32),
            pltpu.VMEM((2, k1_count * 2 * box_edge, grid_len), F32),
            pltpu.VMEM((2, grid_len * 2 * k1_count, grid_len), F32),
            pltpu.VMEM((3, cells, lanes), F32),
            pltpu.VMEM((2 * box_edge, 2 * k1_count), BF16),
            pltpu.VMEM((2, 2 * box_edge, 2 * k1_count), BF16),
            pltpu.VMEM((2 * grid_len, lanes), BF16),
            pltpu.VMEM((2, 2 * grid_len, lanes), BF16),
        ],
        compiler_params=pltpu.CompilerParams(vmem_limit_bytes=60 * 1024 * 1024),
        name="pair_terms",
    )(displace, slab_index, boxes, kernel.reshape(grid_len * k1_count, grid_len), *tables)


def per_device(orbitals, partners, offsets, kernel):
    slab_count = lax.axis_size("slab")
    spread = lax.axis_size("orb")
    orbit_index = lax.axis_index("orb")
    slab_index = lax.axis_index("slab")
    slab_rows = orbitals.shape[1]

    corners = lax.all_gather(offsets, "orb", axis=0, tiled=True)
    held = [orbitals] + [passed_along(orbitals, "orb", -hop) for hop in range(1, REACH + 1)]
    held = jnp.concatenate(held, 0)
    partner_ids = partners.reshape(2)
    hop_of_pair = (partner_ids - orbit_index) % spread
    displace = corners[partner_ids] - offsets
    sent = jnp.concatenate([orbitals, held[hop_of_pair]], 0)
    boxes = lax.all_gather(sent, "slab", axis=1, tiled=True)

    terms = pair_terms(boxes, displace, slab_index[None], kernel, slab_count)

    terms = terms.reshape(3, slab_count, slab_rows, terms.shape[2])
    arrived = lax.all_to_all(terms, "slab", split_axis=1, concat_axis=1, tiled=True)
    total = arrived.astype(F32).sum(1)
    result = total[0]
    far = total[1:].astype(BF16)
    for hop in range(1, REACH + 1):
        bucket = jnp.where(hop_of_pair[0] == hop, far[0], jnp.where(hop_of_pair[1] == hop, far[1], jnp.zeros_like(far[0])))
        result = result + passed_along(bucket, "orb", hop).astype(F32)
    return result[None]


def solution(mesh):
    return jax.shard_map(
        per_device,
        mesh=mesh,
        in_specs=(P("orb", "slab", None), P("orb", None), P("orb", None), P(None, "slab", None)),
        out_specs=P("orb", "slab", None),
        check_vma=False,
    )
```

time: 370 us -> 183 us (0.49)
  the two profiles are of different devices: /device:TPU:0 before, /device:TPU:5 now
where the time goes in v1:
time: 183 us
  Pallas kernels  62.6 us (34%)
  waiting for transfers between devices  47.2 us (26%)
  blocking collectives  30.3 us (17%)
  between operations  18.7 us (10%)
  starting transfers between devices  14.8 us (8%)
  local copies, waits for them, and re-layouts  5.57 us (3%)
  other arithmetic  3.62 us (2%)
    pallas_call x1, Pallas kernels, pair_terms(): pl.pallas_call(functools.partial(pair_kernel, box_edge, k1_count), out_sh...  62.6 us
    all_gather x1, blocking collectives, per_device(): corners = lax.all_gather(offsets, 'orb', axis=0, tiled=True)  30.3 us
    ppermute x8, waiting for transfers between devices, passed_along(): return lax.ppermute(block, axis, route)  26.2 us
    all_to_all x1, waiting for transfers between devices, per_device(): lax.all_to_all(terms, 'slab', split_axis=1, concat_axis=1, tiled=True)  12.8 us
    ppermute x8, starting transfers between devices, passed_along(): return lax.ppermute(block, axis, route)  11 us
    all_gather x1, waiting for transfers between devices, per_device(): boxes = lax.all_gather(sent, 'slab', axis=1, tiled=True)  8.17 us
    all_to_all x1, starting transfers between devices, per_device(): lax.all_to_all(terms, 'slab', split_axis=1, concat_axis=1, tiled=True)  3.8 us
  transfers between devices with their start and end apart: 10, of which 10 were waited for; matrix products, arithmetic and copies ran while one was open for 2% of the time, Pallas kernels for 0%

profile of v1, /device:TPU:5, one launch (start us, length us, event | category | flops | bytes accessed | tf_op | source)
XLA Modules:
  0.0 182.8 jit_solution(11951397065704083900)
XLA Ops:
  6.5 0.0 all-gather.3.cloned.1.call-start
  6.5 0.7 collective-permute-start
  7.2 0.0 collective-permute-start.1
  7.2 4.7 %collective-permute-start.2 = (bf16[1,32,4096]{2,1,0:T(8,128)(2,1)}, bf16[1,32,4096]{2,1,0:T(8,128)(2,1)S(1)}, u32[]{:S(2)}, u32[]{:S(2)}) collective-permute-start(bf16[1,32,4096]{2,1,0:T(8,128)(2,1)} %param.10), channel_id=1, source_target_pairs={{6,0},{8,2},{10,4},{12,6},{14,8},{16,10},{18,12},{20,14},{22,16},{... | collective-permute-start | bytes 786440 | tf_op jit(solution)/shard_map/ppermute | solution.py:21
  11.9 0.2 collective-permute-start.3
  12.1 1.0 constant_dynamic-update-slice_fusion.4
  13.1 0.7 fusion.8
  13.7 2.4 %collective-permute-done = bf16[1,32,4096]{2,1,0:T(8,128)(2,1)S(1)} collective-permute-done((bf16[1,32,4096]{2,1,0:T(8,128)(2,1)}, bf16[1,32,4096]{2,1,0:T(8,128)(2,1)S(1)}, u32[]{:S(2)}, u32[]{:S(2)}) %collective-permute-start) | collective-permute-done | bytes 262176 | tf_op jit(solution)/shard_map/ppermute | solution.py:21
  16.2 0.0 copy-start
  16.2 0.5 collective-permute-done.1
  16.7 2.4 %collective-permute-done.2 = bf16[1,32,4096]{2,1,0:T(8,128)(2,1)S(1)} collective-permute-done((bf16[1,32,4096]{2,1,0:T(8,128)(2,1)}, bf16[1,32,4096]{2,1,0:T(8,128)(2,1)S(1)}, u32[]{:S(2)}, u32[]{:S(2)}) %collective-permute-start.2) | collective-permute-done | bytes 262176 | tf_op jit(solution)/shard_map/ppermute | solution.py:21
  19.1 1.0 collective-permute-done.3
  20.1 0.6 gather_fusion.1
  20.7 0.0 copy-done
  20.7 0.0 copy-start.1
  20.8 1.0 pad_maximum_fusion
  21.7 0.0 all-gather.3.cloned.1.call-update
  21.8 0.0 copy-done.1
  21.8 30.3 %all-gather = s32[16,1,3]{2,1,0:T(1,128)S(1)} all-gather(s32[1,1,3]{2,1,0:T(1,128)S(1)} %bitcast.50), channel_id=1, replica_groups=mesh['orb'=16,'slab'=2] {'orb'}, dimensions={0}, use_global_device_ids=true | all-gather | bytes 204 | tf_op jit(solution)/shard_map/all_gather | solution.py:229
  52.1 0.6 gather_fusion
  52.7 0.6 broadcast_subtract_fusion.shift_ref
  53.2 8.2 %all-gather.3.cloned.1.call-done.boxes_ref = bf16[3,64,4096]{2,1,0:T(8,128)(2,1)} async-done(((bf16[3,32,4096]{2,1,0:T(8,128)(2,1)}), bf16[3,64,4096]{2,1,0:T(8,128)(2,1)}) %all-gather.3.cloned.1.call-update) | async-done | bytes 1572880 | tf_op jit(solution)/shard_map/all_gather | solution.py:236
  61.4 62.6 %pair_terms.1 = bf16[3,64,4096]{2,1,0:T(8,128)(2,1)} custom-call(s32[2,3]{1,0:T(2,128)} %broadcast_subtract_fusion.shift_ref, s32[1]{0:T(128)} %bitcast.5.slab_ref, bf16[3,64,4096]{2,1,0:T(8,128)(2,1)} %all-gather.3.cloned.1.call-done.boxes_ref, f32[8192,128]{1,0:T(8,128)} %bitcast.48, bf16[128,256]{1,0:T(8,128)(2,1)} %constant.61.clone.f2_ref, ...), custom_call_target="tpu_custom_call" | custom-call | tf_op jit(solution)/shard_map/pair_terms/pallas_call | solution.py:201
  124.0 2.7 %copy.15 = bf16[3,2,32,4096]{3,2,0,1:T(8,128)(2,1)} copy(bf16[3,2,32,4096]{3,2,1,0:T(8,128)(2,1)} %bitcast.47) | data formatting | bytes 3145728 | tf_op jit(solution)/shard_map/reshape | solution.py:240
  126.8 0.0 copy-start.2
  126.8 3.8 %all-to-all-start = ((bf16[3,2,32,4096]{3,2,0,1:T(8,128)(2,1)}), bf16[3,2,32,4096]{3,2,0,1:T(8,128)(2,1)S(1)}, u32[]{:S(2)}, u32[]{:S(2)}) async-start(bf16[3,2,32,4096]{3,2,0,1:T(8,128)(2,1)} %copy.15), calls=%async_computation | async-start | bytes 3145728 | tf_op jit(solution)/shard_map/all_to_all | solution.py:241
  130.6 0.0 copy-done.2
  130.6 0.6 fusion.9
  136.3 12.8 %all-to-all-done = bf16[3,2,32,4096]{3,2,0,1:T(8,128)(2,1)S(1)} async-done(((bf16[3,2,32,4096]{3,2,0,1:T(8,128)(2,1)}), bf16[3,2,32,4096]{3,2,0,1:T(8,128)(2,1)S(1)}, u32[]{:S(2)}, u32[]{:S(2)}) %all-to-all-start) | async-done | bytes 1572896 | tf_op jit(solution)/shard_map/all_to_all | solution.py:241
  149.2 0.3 convert_reduce_fusion
  149.5 0.1 convert.3
  149.6 0.1 select_bitcast_fusion.3
  149.6 2.7 %collective-permute-start.4 = (bf16[32,4096]{1,0:T(8,128)(2,1)S(1)}, bf16[32,4096]{1,0:T(8,128)(2,1)S(1)}, u32[]{:S(2)}, u32[]{:S(2)}) collective-permute-start(bf16[32,4096]{1,0:T(8,128)(2,1)S(1)} %get-tuple-element.5), channel_id=1, source_target_pairs={{30,0},{0,2},{2,4},{4,6},{6,8},{8,10},{10,12},{12,14},{14,16},{16,... | collective-permute-start | bytes 786440 | tf_op jit(solution)/shard_map/ppermute | solution.py:21
  152.3 1.2 collective-permute-start.5
  153.5 0.4 collective-permute-start.6
  153.9 1.2 collective-permute-start.7
  155.1 2.8 %collective-permute-done.4 = bf16[32,4096]{1,0:T(8,128)(2,1)S(1)} collective-permute-done((bf16[32,4096]{1,0:T(8,128)(2,1)S(1)}, bf16[32,4096]{1,0:T(8,128)(2,1)S(1)}, u32[]{:S(2)}, u32[]{:S(2)}) %collective-permute-start.4) | collective-permute-done | bytes 262176 | tf_op jit(solution)/shard_map/ppermute | solution.py:21
  157.9 6.3 %collective-permute-done.5 = bf16[32,4096]{1,0:T(8,128)(2,1)S(1)} collective-permute-done((bf16[32,4096]{1,0:T(8,128)(2,1)S(1)}, bf16[32,4096]{1,0:T(8,128)(2,1)S(1)}, u32[]{:S(2)}, u32[]{:S(2)}) %collective-permute-start.5) | collective-permute-done | bytes 262176 | tf_op jit(solution)/shard_map/ppermute | solution.py:21
  164.2 4.9 %collective-permute-done.6 = bf16[32,4096]{1,0:T(8,128)(2,1)S(1)} collective-permute-done((bf16[32,4096]{1,0:T(8,128)(2,1)S(1)}, bf16[32,4096]{1,0:T(8,128)(2,1)S(1)}, u32[]{:S(2)}, u32[]{:S(2)}) %collective-permute-start.6) | collective-permute-done | bytes 262176 | tf_op jit(solution)/shard_map/ppermute | solution.py:21
  169.1 5.9 %collective-permute-done.7 = bf16[32,4096]{1,0:T(8,128)(2,1)S(1)} collective-permute-done((bf16[32,4096]{1,0:T(8,128)(2,1)S(1)}, bf16[32,4096]{1,0:T(8,128)(2,1)S(1)}, u32[]{:S(2)}, u32[]{:S(2)}) %collective-permute-start.7) | collective-permute-done | bytes 262176 | tf_op jit(solution)/shard_map/ppermute | solution.py:21
  175.0 0.9 fusion.4
  (7 shorter events, 0.1 us)
Async XLA Ops:
  6.5 54.9 %all-gather.3.cloned.1.call-start = ((), (), s32[]{:S(2)}) async-start(), calls=%async_computation.1 | async-start | bytes 2359296 | tf_op jit(solution)/shard_map/all_gather | solution.py:236
  6.5 9.6 %collective-permute-start = (bf16[1,32,4096]{2,1,0:T(8,128)(2,1)}, bf16[1,32,4096]{2,1,0:T(8,128)(2,1)S(1)}, u32[]{:S(2)}, u32[]{:S(2)}) collective-permute-start(bf16[1,32,4096]{2,1,0:T(8,128)(2,1)} %param.10), channel_id=1, source_target_pairs={{2,0},{4,2},{6,4},{8,6},{10,8},{12,10},{14,12},{16,14},{18,16},{20... | collective-permute-start | bytes 786440 | tf_op jit(solution)/shard_map/ppermute | solution.py:21
  7.2 9.4 %collective-permute-start.1 = (bf16[1,32,4096]{2,1,0:T(8,128)(2,1)}, bf16[1,32,4096]{2,1,0:T(8,128)(2,1)S(1)}, u32[]{:S(2)}, u32[]{:S(2)}) collective-permute-start(bf16[1,32,4096]{2,1,0:T(8,128)(2,1)} %param.10), channel_id=1, source_target_pairs={{4,0},{6,2},{8,4},{10,6},{12,8},{14,10},{16,12},{18,14},{20,16},{2... | collective-permute-start | bytes 786440 | tf_op jit(solution)/shard_map/ppermute | solution.py:21
  7.2 11.9 %collective-permute-start.2 = (bf16[1,32,4096]{2,1,0:T(8,128)(2,1)}, bf16[1,32,4096]{2,1,0:T(8,128)(2,1)S(1)}, u32[]{:S(2)}, u32[]{:S(2)}) collective-permute-start(bf16[1,32,4096]{2,1,0:T(8,128)(2,1)} %param.10), channel_id=1, source_target_pairs={{6,0},{8,2},{10,4},{12,6},{14,8},{16,10},{18,12},{20,14},{22,16},{... | collective-permute-start | bytes 786440 | tf_op jit(solution)/shard_map/ppermute | solution.py:21
  11.9 8.2 %collective-permute-start.3 = (bf16[1,32,4096]{2,1,0:T(8,128)(2,1)}, bf16[1,32,4096]{2,1,0:T(8,128)(2,1)S(1)}, u32[]{:S(2)}, u32[]{:S(2)}) collective-permute-start(bf16[1,32,4096]{2,1,0:T(8,128)(2,1)} %param.10), channel_id=1, source_target_pairs={{8,0},{10,2},{12,4},{14,6},{16,8},{18,10},{20,12},{22,14},{24,16},... | collective-permute-start | bytes 786440 | tf_op jit(solution)/shard_map/ppermute | solution.py:21
  16.2 4.6 %copy-start = (bf16[1,32,4096]{2,1,0:T(8,128)(2,1)S(1)}, bf16[1,32,4096]{2,1,0:T(8,128)(2,1)}, u32[]{:S(2)}) copy-start(bf16[1,32,4096]{2,1,0:T(8,128)(2,1)} %param.10) | copy-start | bytes 786436
  20.7 1.0 copy-start.1
  126.8 3.8 %copy-start.2 = (s32[1,2]{1,0:T(1,128)S(1)}, s32[1,2]{1,0:T(1,128)}, u32[]{:S(2)}) copy-start(s32[1,2]{1,0:T(1,128)} %param.11) | copy-start | bytes 28
  126.8 22.4 %all-to-all-start = ((bf16[3,2,32,4096]{3,2,0,1:T(8,128)(2,1)}), bf16[3,2,32,4096]{3,2,0,1:T(8,128)(2,1)S(1)}, u32[]{:S(2)}, u32[]{:S(2)}) async-start(bf16[3,2,32,4096]{3,2,0,1:T(8,128)(2,1)} %copy.15), calls=%async_computation | async-start | bytes 3145728 | tf_op jit(solution)/shard_map/all_to_all | solution.py:241
  149.6 8.2 %collective-permute-start.4 = (bf16[32,4096]{1,0:T(8,128)(2,1)S(1)}, bf16[32,4096]{1,0:T(8,128)(2,1)S(1)}, u32[]{:S(2)}, u32[]{:S(2)}) collective-permute-start(bf16[32,4096]{1,0:T(8,128)(2,1)S(1)} %get-tuple-element.5), channel_id=1, source_target_pairs={{30,0},{0,2},{2,4},{4,6},{6,8},{8,10},{10,12},{12,14},{14,16},{16,... | collective-permute-start | bytes 786440 | tf_op jit(solution)/shard_map/ppermute | solution.py:21
  152.3 11.9 %collective-permute-start.5 = (bf16[32,4096]{1,0:T(8,128)(2,1)S(1)}, bf16[32,4096]{1,0:T(8,128)(2,1)S(1)}, u32[]{:S(2)}, u32[]{:S(2)}) collective-permute-start(bf16[32,4096]{1,0:T(8,128)(2,1)S(1)} %get-tuple-element.8), channel_id=1, source_target_pairs={{28,0},{30,2},{0,4},{2,6},{4,8},{6,10},{8,12},{10,14},{12,16},{14,... | collective-permute-start | bytes 786440 | tf_op jit(solution)/shard_map/ppermute | solution.py:21
  153.5 15.6 %collective-permute-start.6 = (bf16[32,4096]{1,0:T(8,128)(2,1)S(1)}, bf16[32,4096]{1,0:T(8,128)(2,1)S(1)}, u32[]{:S(2)}, u32[]{:S(2)}) collective-permute-start(bf16[32,4096]{1,0:T(8,128)(2,1)S(1)} %get-tuple-element.6), channel_id=1, source_target_pairs={{26,0},{28,2},{30,4},{0,6},{2,8},{4,10},{6,12},{8,14},{10,16},{12,... | collective-permute-start | bytes 786440 | tf_op jit(solution)/shard_map/ppermute | solution.py:21
  153.9 21.1 %collective-permute-start.7 = (bf16[32,4096]{1,0:T(8,128)(2,1)S(1)}, bf16[32,4096]{1,0:T(8,128)(2,1)S(1)}, u32[]{:S(2)}, u32[]{:S(2)}) collective-permute-start(bf16[32,4096]{1,0:T(8,128)(2,1)S(1)} %get-tuple-element.7), channel_id=1, source_target_pairs={{24,0},{26,2},{28,4},{30,6},{0,8},{2,10},{4,12},{6,14},{8,16},{10,... | collective-permute-start | bytes 786440 | tf_op jit(solution)/shard_map/ppermute | solution.py:21
Sparse Core Ops, SparseCore 0:
  21.9 39.4 all-gather.2

commit v2 on v1

v2 whole, which is shorter than its diff:
```python
import functools
import math

import jax
import jax.numpy as jnp
import ml_dtypes
import numpy as np
from jax import lax
from jax.experimental import pallas as pl
from jax.experimental.pallas import tpu as pltpu
from jax.sharding import PartitionSpec as P

REACH = 4
F32 = jnp.float32
BF16 = jnp.bfloat16


def phases(places, frequency, grid_len, signed):
    wrapped = (places[:, None] * frequency[None, :]) % grid_len
    angles = wrapped.astype(np.float64) * (2.0 * math.pi / grid_len)
    return np.cos(angles), signed * np.sin(angles)


def block_form(cos, sin):
    return np.block([[cos, -sin], [sin, cos]])


def make_tables(box_edge, slab_count):
    grid_len = 2 * box_edge
    half = box_edge // 2
    k1_count = grid_len // slab_count
    box = np.arange(box_edge) + half
    grid = np.arange(grid_len)
    cos, sin = phases(box, grid, grid_len, -1.0)
    f2 = np.zeros((2 * box_edge, 2 * grid_len))
    f2[:box_edge] = np.concatenate([cos, sin], 1)
    f0 = block_form(cos.T, sin.T)
    f1 = []
    e1 = []
    gcos, gsin = phases(grid, grid, grid_len, 1.0)
    for s in range(slab_count):
        mine = slice(s * k1_count, (s + 1) * k1_count)
        f1.append(block_form(cos.T[mine], sin.T[mine]))
        e1.append(block_form(gcos[:, mine], gsin[:, mine]))
    e0 = block_form(gcos, gsin)
    e2 = np.concatenate([gcos.T, -gsin.T], 0) / grid_len**3
    tables = [f2, np.stack(f1), f0, e0, np.stack(e1), e2]
    return [t.astype(np.float32).astype(ml_dtypes.bfloat16) for t in tables]


def dot(a, b):
    return jnp.dot(a, b, preferred_element_type=F32)


def pair_kernel(
    box_edge, k1_count,
    slab_ref,
    boxes_ref, kernel_ref, f2_ref, f1_ref, f0_ref, e0_ref, e1_ref, e2_ref,
    out_ref,
    cells, here, y_parts, v_parts, terms, e1_own, e1_far, e2_own, e2_far,
):
    edge = box_edge
    grid_len = 2 * edge
    half = edge // 2
    lanes = 2 * edge
    slab_count = boxes_ref.shape[0]
    slab = slab_ref[0]
    lane = lax.broadcasted_iota(jnp.int32, (edge, lanes), 1)
    low_lanes = lane < edge
    row = lax.broadcasted_iota(jnp.int32, (edge, lanes), 0)
    corner_lane = lax.broadcasted_iota(jnp.int32, (1, lanes), 1)

    def corner(b):
        held = boxes_ref[0, b, :, pl.ds(edge * edge, lanes)].astype(F32)[0:1]
        return [jnp.sum(jnp.where(corner_lane == c, held, 0.0)).astype(jnp.int32) for c in range(3)]

    corners = [corner(b) for b in range(3)]
    shifts = [[corners[1 + n][c] - corners[0][c] for c in range(3)] for n in range(2)]
    cell_pitch = edge + 1
    y_pitch = 2 * edge + 1
    v_pitch = 2 * k1_count + 1

    e1_grid = e1_ref[slab]
    e2_grid = e2_ref[...]
    sel_lane = lax.broadcasted_iota(jnp.int32, (grid_len, lanes), 1)
    sel_row = lax.broadcasted_iota(jnp.int32, (grid_len, lanes), 0)

    def windows(d1, d2):
        pick_rows = (row + half + d1 == lane).astype(F32).astype(BF16)
        top = dot(pick_rows, e1_grid[:grid_len]).astype(BF16)
        bottom = dot(pick_rows, e1_grid[grid_len:]).astype(BF16)
        pick_cols = ((sel_lane + half + d2 == sel_row) & (sel_lane < edge)).astype(F32).astype(BF16)
        return jnp.concatenate([top, bottom], 0), dot(e2_grid, pick_cols).astype(BF16)

    e1_own[...], e2_own[...] = windows(0, 0)
    for n in range(2):
        e1_far[n], e2_far[n] = windows(shifts[n][1], shifts[n][2])

    def unpack(g, carry):
        lo_at = pl.ds(2 * g, edge, stride=cell_pitch)
        hi_at = pl.ds(2 * g + 1, edge, stride=cell_pitch)
        for b in range(3):
            both = boxes_ref[:, b, :, pl.ds(pl.multiple_of(g * lanes, lanes), lanes)].astype(F32)
            both = both.reshape(edge, lanes)
            cells[b, lo_at, :] = jnp.where(low_lanes, both, 0.0)
            cells[b, hi_at, :] = jnp.where(low_lanes, pltpu.roll(both, edge, 1), 0.0)
        return carry

    lax.fori_loop(0, edge // 2, unpack, 0, unroll=2)

    def moved(b, c0, d0, d1, d2):
        source = c0 + d0
        at = jnp.clip(source, 0, edge - 1)
        block = cells[b, pl.ds(at * cell_pitch, edge), :]
        block = pltpu.roll(block, (-d2) & (lanes - 1), 1)
        block = pltpu.roll(block, (-d1) & (edge - 1), 0)
        inside = (row + d1 >= 0) & (row + d1 < edge) & (source >= 0) & (source < edge)
        return jnp.where(inside, block, 0.0)

    def forward(c0, carry):
        at = pl.ds(pl.multiple_of(c0 * edge, edge), edge)
        own = cells[0, pl.ds(c0 * cell_pitch, edge), :]
        z = []
        for n in range(2):
            d0, d1, d2 = shifts[n]
            partner = moved(1 + n, c0, -d0, -d1, -d2)
            here[n, at, :] = partner
            z.append((own * partner).astype(BF16))
        z = dot(jnp.concatenate(z, 0), f2_ref[...]).astype(BF16)
        z = jnp.concatenate(
            [
                jnp.concatenate([z[n * edge : (n + 1) * edge, :grid_len], z[n * edge : (n + 1) * edge, grid_len:]], 0)
                for n in range(2)
            ],
            1,
        )
        y = dot(f1_ref[slab], z)
        for n in range(2):
            part = y[:, n * grid_len : (n + 1) * grid_len]
            y_parts[n, pl.ds(c0, k1_count, stride=y_pitch), :] = part[:k1_count]
            y_parts[n, pl.ds(edge + c0, k1_count, stride=y_pitch), :] = part[k1_count:]
        return carry

    lax.fori_loop(0, edge, forward, 0, unroll=4)

    def middle(k1, carry):
        at = pl.ds(k1 * y_pitch, 2 * edge)
        y = jnp.concatenate([y_parts[n, at, :].astype(BF16) for n in range(2)], 1)
        x = dot(f0_ref[...], y)
        k = kernel_ref[pl.ds(k1, grid_len, stride=k1_count), :]
        k = jnp.concatenate([k, k], 1)
        w = jnp.concatenate([(x[:grid_len] * k).astype(BF16), (x[grid_len:] * k).astype(BF16)], 0)
        v = dot(e0_ref[...], w)
        for n in range(2):
            part = v[:, n * grid_len : (n + 1) * grid_len]
            v_parts[n, pl.ds(k1, grid_len, stride=v_pitch), :] = part[:grid_len]
            v_parts[n, pl.ds(k1_count + k1, grid_len, stride=v_pitch), :] = part[grid_len:]
        return carry

    lax.fori_loop(0, k1_count, middle, 0, unroll=4)

    def v_rows(n, u0):
        at = pl.ds(u0 * v_pitch, 2 * k1_count)
        return v_parts[n, at, :].astype(BF16)

    def backward(c0, carry):
        at = pl.ds(pl.multiple_of(c0 * edge, edge), edge)
        v = jnp.concatenate([v_rows(n, half + c0) for n in range(2)], 1)
        u = dot(e1_own[...], v).astype(BF16)
        u = jnp.concatenate(
            [
                jnp.concatenate([u[:edge, n * grid_len : (n + 1) * grid_len], u[edge:, n * grid_len : (n + 1) * grid_len]], 1)
                for n in range(2)
            ],
            0,
        )
        field = dot(u, e2_own[...])
        to = pl.ds(c0 * cell_pitch, edge)
        terms[0, to, :] = field[:edge] * here[0, at, :] + field[edge:] * here[1, at, :]
        for n in range(2):
            d0, d1, d2 = shifts[n]
            u = dot(e1_far[n], v_rows(n, half + d0 + c0)).astype(BF16)
            field = dot(jnp.concatenate([u[:edge], u[edge:]], 1), e2_far[n])
            terms[1 + n, to, :] = field * moved(0, c0, d0, d1, d2)
        return carry

    lax.fori_loop(0, edge, backward, 0, unroll=4)

    def pack(g, carry):
        for b in range(3):
            lo = terms[b, pl.ds(2 * g, edge, stride=cell_pitch), :]
            hi = terms[b, pl.ds(2 * g + 1, edge, stride=cell_pitch), :]
            both = (lo + pltpu.roll(hi, edge, 1)).reshape(slab_count, edge // slab_count, lanes)
            out_ref[:, b, :, pl.ds(pl.multiple_of(g * lanes, lanes), lanes)] = both.astype(BF16)
        return carry

    lax.fori_loop(0, edge // 2, pack, 0, unroll=2)


def pair_terms(boxes, slab_index, kernel):
    slab_count, _, rows, _ = boxes.shape
    box_edge = slab_count * rows
    grid_len, k1_count = kernel.shape[0], kernel.shape[1]
    tables = make_tables(box_edge, slab_count)
    smem = pl.BlockSpec(memory_space=pltpu.SMEM)
    vmem = pl.BlockSpec(memory_space=pltpu.VMEM)
    cells = box_edge * box_edge
    cell_rows = box_edge * (box_edge + 1)
    lanes = 2 * box_edge
    return pl.pallas_call(
        functools.partial(pair_kernel, box_edge, k1_count),
        out_shape=jax.ShapeDtypeStruct((slab_count, 3, rows, cells), BF16),
        in_specs=[smem] + [vmem] * 8,
        out_specs=vmem,
        scratch_shapes=[
            pltpu.VMEM((3, cell_rows, lanes), F32),
            pltpu.VMEM((2, cells, lanes), F32),
            pltpu.VMEM((2, k1_count * (2 * box_edge + 1), grid_len), F32),
            pltpu.VMEM((2, grid_len * (2 * k1_count + 1), grid_len), F32),
            pltpu.VMEM((3, cell_rows, lanes), F32),
            pltpu.VMEM((2 * box_edge, 2 * k1_count), BF16),
            pltpu.VMEM((2, 2 * box_edge, 2 * k1_count), BF16),
            pltpu.VMEM((2 * grid_len, lanes), BF16),
            pltpu.VMEM((2, 2 * grid_len, lanes), BF16),
        ],
        compiler_params=pltpu.CompilerParams(vmem_limit_bytes=60 * 1024 * 1024),
        name="pair_terms",
    )(slab_index, boxes, kernel.reshape(grid_len * k1_count, grid_len), *tables)


def neighbours(orb_count):
    i = lax.axis_index("orb")
    core, side = lax.rem(i, 2), lax.rem(i // 2, 2)
    sibling = i + 1 - 2 * core
    across = i + 2 - 4 * side
    behind = lax.rem(i + orb_count - REACH, orb_count)
    ahead = lax.rem(i + REACH, orb_count)
    return i, core, side, sibling, across, behind, ahead


def slot_of(partner, i, side, orb_count):
    hop = jnp.minimum(lax.rem(partner - i + orb_count, orb_count), REACH)
    target = lax.rem(i, REACH) + hop
    group, place = target // REACH, lax.rem(target, REACH)
    return 2 * jnp.where(place // 2 == side, group, 2) + lax.rem(place, 2)


def remote(src, dst, send_sem, recv_sem, orb, slab):
    return pltpu.make_async_remote_copy(
        src_ref=src, dst_ref=dst, send_sem=send_sem, recv_sem=recv_sem,
        device_id=(orb, slab), device_id_type=pl.DeviceIdType.MESH,
    )


def greet(peers):
    barrier = pltpu.get_barrier_semaphore()
    for peer in peers:
        pl.semaphore_signal(barrier, inc=1, device_id=peer, device_id_type=pl.DeviceIdType.MESH)
    pl.semaphore_wait(barrier, len(peers))


def gather_kernel(
    orb_count, slab_count, chunks,
    partners_ref, offsets_ref, orbital_ref, out_ref,
    z_send, z_recv, y_send, y_recv, core_send, core_recv, own_send, own_recv, pick_send, pick_recv,
    *held,
):
    i, core, side, sibling, across, behind, ahead = neighbours(orb_count)
    s = lax.axis_index("slab")
    others = [lax.rem(s + k, slab_count) for k in range(1, slab_count)]
    rows, cells = orbital_ref.shape
    width = out_ref.shape[3] // chunks
    cols = [pl.ds(q * width, width) for q in range(chunks)]

    lane = lax.broadcasted_iota(jnp.int32, (rows, 128), 1)
    corner = jnp.zeros((rows, 128), F32)
    for c in range(3):
        corner = jnp.where(lane == c, offsets_ref[0, c].astype(F32), corner)
    out_ref[s, 0, :, pl.ds(0, cells)] = orbital_ref[...]
    out_ref[s, 0, :, pl.ds(cells, 128)] = corner.astype(BF16)
    for q in range(chunks):
        held[q][core] = out_ref[s, 0, :, cols[q]]
    greet([(p, s) for p in (sibling, across, behind, ahead)] + [(i, o) for o in others])

    z = [remote(held[q].at[core], held[q].at[2 + core], z_send.at[q], z_recv.at[q], behind, s) for q in range(chunks)]
    by_core = [
        [
            remote(held[q].at[2 * g + core], held[q].at[2 * g + core], core_send.at[g, q], core_recv.at[g, q], sibling, s)
            for q in range(chunks)
        ]
        for g in range(3)
    ]
    y_here = [remote(held[q].at[core], held[q].at[4 + core], y_send.at[q], y_recv.at[q], across, s) for q in range(chunks)]
    y_pass = [remote(held[q].at[2 + core], held[q].at[4 + core], y_send.at[q], y_recv.at[q], across, s) for q in range(chunks)]
    own = [
        remote(out_ref.at[s, 0], out_ref.at[s, 0], own_send.at[k], own_recv.at[k], i, o) for k, o in enumerate(others)
    ]
    for q in range(chunks):
        z[q].start()
    for q in range(chunks):
        pl.when(side == 1)(y_here[q].start)
    for copy in own:
        copy.start()
    for q in range(chunks):
        by_core[0][q].start()
    for q in range(chunks):
        z[q].wait_recv()
        pl.when(side == 0)(y_pass[q].start)
        by_core[1][q].start()
    slots = [slot_of(partners_ref[0, n], i, side, orb_count) for n in range(2)]
    picks = []
    for q in range(chunks):
        y_here[q].wait_recv()
        by_core[2][q].start()
        for g in range(3):
            by_core[g][q].wait_recv()
        for n in range(2):
            out_ref[s, 1 + n, :, cols[q]] = held[q][slots[n]]
            for k, o in enumerate(others):
                here = out_ref.at[s, 1 + n, :, cols[q]]
                picks.append(remote(here, here, pick_send.at[n, q, k], pick_recv.at[n, q, k], i, o))
                picks[-1].start()
    for q in range(chunks):
        z[q].wait_send()
        y_here[q].wait_send()
        for g in range(3):
            by_core[g][q].wait_send()
    for copy in own + picks:
        copy.wait()


def gather_boxes(orbitals, partners, offsets):
    orb_count, slab_count = lax.axis_size("orb"), lax.axis_size("slab")
    rows, cells = orbitals.shape[1:]
    lanes = cells + 128
    chunks = 3 if lanes % (3 * 128) == 0 else 1
    smem = pl.BlockSpec(memory_space=pltpu.SMEM)
    vmem = pl.BlockSpec(memory_space=pltpu.VMEM)
    dma = pltpu.SemaphoreType.DMA
    peers = slab_count - 1
    return pl.pallas_call(
        functools.partial(gather_kernel, orb_count, slab_count, chunks),
        out_shape=jax.ShapeDtypeStruct((slab_count, 3, rows, lanes), BF16),
        in_specs=[smem, smem, vmem],
        out_specs=vmem,
        scratch_shapes=[
            dma((chunks,)), dma((chunks,)), dma((chunks,)), dma((chunks,)),
            dma((3, chunks)), dma((3, chunks)), dma((peers,)), dma((peers,)),
            dma((2, chunks, peers)), dma((2, chunks, peers)),
        ] + [pltpu.VMEM((6, rows, lanes // chunks), BF16)] * chunks,
        compiler_params=pltpu.CompilerParams(
            collective_id=0, has_side_effects=True, vmem_limit_bytes=32 * 1024 * 1024
        ),
        name="gather_boxes",
    )(partners, offsets, orbitals.reshape(rows, cells))


def scatter_kernel(
    orb_count, slab_count, chunks,
    partners_ref, terms_ref, out_ref,
    x_send, x_recv, core_send, core_recv, y_send, y_recv, z_send, z_recv,
    from_slab, kept, to_core, from_core, to_y, from_y, to_z, from_z,
):
    i, core, side, sibling, across, behind, ahead = neighbours(orb_count)
    s = lax.axis_index("slab")
    others = [lax.rem(s + k, slab_count) for k in range(1, slab_count)]
    width = out_ref.shape[1] // chunks
    cols = [pl.ds(q * width, width) for q in range(chunks)]
    greet([(p, s) for p in (sibling, across, behind, ahead)] + [(i, o) for o in others])

    x = [
        [
            remote(terms_ref.at[o, :, :, cols[q]], from_slab.at[k, :, :, cols[q]], x_send.at[q, k], x_recv.at[q, k], i, o)
            for k, o in enumerate(others)
        ]
        for q in range(chunks)
    ]
    c = [
        remote(to_core.at[:, :, cols[q]], from_core.at[:, :, cols[q]], core_send.at[q], core_recv.at[q], sibling, s)
        for q in range(chunks)
    ]
    y = [remote(to_y.at[:, cols[q]], from_y.at[:, cols[q]], y_send.at[q], y_recv.at[q], across, s) for q in range(chunks)]
    z = [remote(to_z.at[:, cols[q]], from_z.at[:, cols[q]], z_send.at[q], z_recv.at[q], ahead, s) for q in range(chunks)]
    for q in range(chunks):
        for copy in x[q]:
            copy.start()
    slots = [slot_of(partners_ref[0, n], i, side, orb_count) for n in range(2)]

    def sum_slabs(q):
        for copy in x[q]:
            copy.wait_recv()
        total = [terms_ref[s, b, :, cols[q]].astype(F32) for b in range(3)]
        for k in range(slab_count - 1):
            total = [total[b] + from_slab[k, b, :, cols[q]].astype(F32) for b in range(3)]
        out_ref[:, cols[q]] = total[0]

        def share(slot):
            return jnp.where(slots[0] == slot, total[1], jnp.where(slots[1] == slot, total[2], 0.0))

        for g in range(3):
            to_core[g, :, cols[q]] = share(2 * g + 1 - core).astype(BF16)
        for g in range(1, 3):
            kept[g - 1, :, cols[q]] = share(2 * g + core)
        c[q].start()

    def over_core(q):
        c[q].wait_recv()
        out_ref[:, cols[q]] += from_core[0, :, cols[q]].astype(F32)
        to_y[:, cols[q]] = (kept[1, :, cols[q]] + from_core[2, :, cols[q]].astype(F32)).astype(BF16)
        y[q].start()
        kept[0, :, cols[q]] += from_core[1, :, cols[q]].astype(F32)

    def over_y(q):
        y[q].wait_recv()
        came = from_y[:, cols[q]].astype(F32)
        to_z[:, cols[q]] = (kept[0, :, cols[q]] + jnp.where(side == 0, came, 0.0)).astype(BF16)
        z[q].start()
        out_ref[:, cols[q]] += jnp.where(side == 1, came, 0.0)

    def over_z(q):
        z[q].wait_recv()
        out_ref[:, cols[q]] += from_z[:, cols[q]].astype(F32)

    stages = [sum_slabs, over_core, over_y, over_z]
    for step in range(chunks + len(stages) - 1):
        for position in reversed(range(len(stages))):
            if 0 <= step - position < chunks:
                stages[position](step - position)
    for q in range(chunks):
        for copy in x[q] + [c[q], y[q], z[q]]:
            copy.wait_send()


def scatter_terms(terms, partners):
    orb_count, slab_count = lax.axis_size("orb"), lax.axis_size("slab")
    rows, cells = terms.shape[2:]
    chunks = 4
    smem = pl.BlockSpec(memory_space=pltpu.SMEM)
    vmem = pl.BlockSpec(memory_space=pltpu.VMEM)
    dma = pltpu.SemaphoreType.DMA
    peers = slab_count - 1
    half = (rows, cells)
    return pl.pallas_call(
        functools.partial(scatter_kernel, orb_count, slab_count, chunks),
        out_shape=jax.ShapeDtypeStruct(half, F32),
        in_specs=[smem, vmem],
        out_specs=vmem,
        scratch_shapes=[dma((chunks, peers))] * 2 + [dma((chunks,))] * 6 + [
            pltpu.VMEM((peers, 3) + half, BF16),
            pltpu.VMEM((2,) + half, F32),
            pltpu.VMEM((3,) + half, BF16),
            pltpu.VMEM((3,) + half, BF16),
        ] + [pltpu.VMEM(half, BF16)] * 4,
        compiler_params=pltpu.CompilerParams(
            collective_id=1, has_side_effects=True, vmem_limit_bytes=32 * 1024 * 1024
        ),
        name="scatter_terms",
    )(partners, terms)


def per_device(orbitals, partners, offsets, kernel):
    slab_index = lax.axis_index("slab").astype(jnp.int32)
    boxes = gather_boxes(orbitals, partners, offsets)
    terms = pair_terms(boxes, slab_index[None], kernel)
    return scatter_terms(terms, partners)[None]


def solution(mesh):
    return jax.shard_map(
        per_device,
        mesh=mesh,
        in_specs=(P("orb", "slab", None), P("orb", None), P("orb", None), P(None, "slab", None)),
        out_specs=P("orb", "slab", None),
        check_vma=False,
    )
```

time: 183 us -> 99.1 us (0.54)
  the two profiles are of different devices: /device:TPU:5 before, /device:TPU:0 now
where the time goes in v2:
time: 99.1 us; the launch traced here: 98.9 us
  Pallas kernels  93.2 us (94%)
  local copies, waits for them, and re-layouts  5.63 us (6%)
    pallas_call x1, Pallas kernels, pair_terms(): pl.pallas_call(functools.partial(pair_kernel, box_edge, k1_count), out_sh...  34.8 us
    pallas_call x1, Pallas kernels, scatter_terms(): pl.pallas_call(functools.partial(scatter_kernel, orb_count, slab_count, c...  32.6 us
    pallas_call x1, Pallas kernels, gather_boxes(): pl.pallas_call(functools.partial(gather_kernel, orb_count, slab_count, ch...  25.8 us
    unnamed x13, local copies, waits for them, and re-layouts  5.63 us

profile of v2, /device:TPU:0, one launch (start us, length us, event | category | flops | bytes accessed | tf_op | source)
XLA Modules:
  0.0 98.9 jit_solution(1501843031554198625)
XLA Ops:
  0.0 0.0 copy-start.2
  0.0 0.9 copy-done.2
  1.0 0.0 copy-start.3
  1.0 0.7 copy-done.3
  1.6 0.0 copy-start.5
  1.6 0.7 copy-done.5
  2.3 25.8 %gather_boxes.1.boxes_ref = bf16[2,3,32,4224]{3,2,1,0:T(8,128)(2,1)S(1)} custom-call(s32[1,2]{1,0:T(1,128)S(1)} %copy-done.3, s32[1,3]{1,0:T(1,128)S(1)} %copy-done.5, bf16[32,4096]{1,0:T(8,128)(2,1)S(1)} %bitcast.5), custom_call_target="tpu_custom_call" | custom-call | tf_op jit(solution)/shard_map/gather_boxes/pallas_call | solution.py:341
  28.0 0.0 copy-start
  28.0 1.2 %copy-done = bf16[2,3,32,4224]{3,2,1,0:T(8,128)(2,1)} copy-done((bf16[2,3,32,4224]{3,2,1,0:T(8,128)(2,1)}, bf16[2,3,32,4224]{3,2,1,0:T(8,128)(2,1)S(1)}, u32[]{:S(2)}) %copy-start) | copy-done | bytes 1622040
  29.2 0.0 copy-start.4
  29.2 34.8 %pair_terms.1.terms_ref = bf16[2,3,32,4096]{3,2,1,0:T(8,128)(2,1)} custom-call(s32[1]{0:T(128)} %bitcast.slab_ref, bf16[2,3,32,4224]{3,2,1,0:T(8,128)(2,1)} %copy-done, f32[8192,128]{1,0:T(8,128)} %bitcast.6, bf16[128,256]{1,0:T(8,128)(2,1)} %constant.16.clone.f2_ref, bf16[2,128,128]{2,1,0:T(8,128)(2,1)} %constant.17.clone.f1_ref, ...), custom_call_target="tpu_custom_call" | custom-call | tf_op jit(solution)/shard_map/pair_terms/pallas_call | solution.py:210
  64.0 0.0 copy-done.4
  64.0 0.0 copy-start.1
  64.0 1.4 %copy-done.1 = bf16[2,3,32,4096]{3,2,1,0:T(8,128)(2,1)S(1)} copy-done((bf16[2,3,32,4096]{3,2,1,0:T(8,128)(2,1)S(1)}, bf16[2,3,32,4096]{3,2,1,0:T(8,128)(2,1)}, u32[]{:S(2)}) %copy-start.1) | copy-done | bytes 1572888
  65.4 32.6 %scatter_terms.1 = f32[32,4096]{1,0:T(8,128)S(1)} custom-call(s32[1,2]{1,0:T(1,128)S(1)} %copy-done.4, bf16[2,3,32,4096]{3,2,1,0:T(8,128)(2,1)S(1)} %copy-done.1), custom_call_target="tpu_custom_call" | custom-call | tf_op jit(solution)/shard_map/scatter_terms/pallas_call | solution.py:443
  98.1 0.8 copy.12
Async XLA Ops:
  0.0 0.9 copy-start.2
  1.0 0.7 copy-start.3
  1.6 0.7 copy-start.5
  28.0 1.2 %copy-start = (bf16[2,3,32,4224]{3,2,1,0:T(8,128)(2,1)}, bf16[2,3,32,4224]{3,2,1,0:T(8,128)(2,1)S(1)}, u32[]{:S(2)}) copy-start(bf16[2,3,32,4224]{3,2,1,0:T(8,128)(2,1)S(1)} %gather_boxes.1.boxes_ref) | copy-start | bytes 4866052
  29.2 34.8 %copy-start.4 = (s32[1,2]{1,0:T(1,128)S(1)}, s32[1,2]{1,0:T(1,128)}, u32[]{:S(2)}) copy-start(s32[1,2]{1,0:T(1,128)} %partners_ref.3) | copy-start | bytes 28
  64.0 1.4 %copy-start.1 = (bf16[2,3,32,4096]{3,2,1,0:T(8,128)(2,1)S(1)}, bf16[2,3,32,4096]{3,2,1,0:T(8,128)(2,1)}, u32[]{:S(2)}) copy-start(bf16[2,3,32,4096]{3,2,1,0:T(8,128)(2,1)} %pair_terms.1.terms_ref) | copy-start | bytes 4718596

commit v3 on v1

v3 whole, which is shorter than its diff:
```python
import functools
import math

import jax
import jax.numpy as jnp
import ml_dtypes
import numpy as np
from jax import lax
from jax.experimental import pallas as pl
from jax.experimental.pallas import tpu as pltpu
from jax.sharding import PartitionSpec as P

REACH = 4
F32 = jnp.float32
BF16 = jnp.bfloat16


def phases(places, frequency, grid_len, signed):
    wrapped = (places[:, None] * frequency[None, :]) % grid_len
    angles = wrapped.astype(np.float64) * (2.0 * math.pi / grid_len)
    return np.cos(angles), signed * np.sin(angles)


def block_form(cos, sin):
    return np.block([[cos, -sin], [sin, cos]])


def make_tables(box_edge, slab_count):
    grid_len = 2 * box_edge
    half = box_edge // 2
    k1_count = grid_len // slab_count
    box = np.arange(box_edge) + half
    grid = np.arange(grid_len)
    cos, sin = phases(box, grid, grid_len, -1.0)
    f2 = np.zeros((2 * box_edge, 2 * grid_len))
    f2[:box_edge] = np.concatenate([cos, sin], 1)
    f0 = block_form(cos.T, sin.T)
    f1 = []
    e1 = []
    gcos, gsin = phases(grid, grid, grid_len, 1.0)
    for s in range(slab_count):
        mine = slice(s * k1_count, (s + 1) * k1_count)
        f1.append(block_form(cos.T[mine], sin.T[mine]))
        e1.append(block_form(gcos[:, mine], gsin[:, mine]))
    e0 = block_form(gcos, gsin)
    e2 = np.concatenate([gcos.T, -gsin.T], 0) / grid_len**3
    tables = [f2, np.stack(f1), f0, e0, np.stack(e1), e2]
    return [t.astype(np.float32).astype(ml_dtypes.bfloat16) for t in tables]


def dot(a, b):
    return jnp.dot(a, b, preferred_element_type=F32)


def neighbours(orb_count):
    i = lax.axis_index("orb")
    core, side = lax.rem(i, 2), lax.rem(i // 2, 2)
    sibling = i + 1 - 2 * core
    across = i + 2 - 4 * side
    behind = lax.rem(i + orb_count - REACH, orb_count)
    ahead = lax.rem(i + REACH, orb_count)
    return i, core, side, sibling, across, behind, ahead


def slot_of(partner, i, side, orb_count):
    hop = jnp.minimum(lax.rem(partner - i + orb_count, orb_count), REACH)
    target = lax.rem(i, REACH) + hop
    group, place = target // REACH, lax.rem(target, REACH)
    return 2 * jnp.where(place // 2 == side, group, 2) + lax.rem(place, 2)


def remote(src, dst, send_sem, recv_sem, orb, slab):
    return pltpu.make_async_remote_copy(
        src_ref=src, dst_ref=dst, send_sem=send_sem, recv_sem=recv_sem,
        device_id=(orb, slab), device_id_type=pl.DeviceIdType.MESH,
    )


def greet(peers):
    barrier = pltpu.get_barrier_semaphore()
    for peer in peers:
        pl.semaphore_signal(barrier, inc=1, device_id=peer, device_id_type=pl.DeviceIdType.MESH)
    pl.semaphore_wait(barrier, len(peers))


def gather_kernel(
    orb_count, slab_count, chunks,
    partners_ref, offsets_ref, orbital_ref, out_ref,
    z_send, z_recv, y_send, y_recv, core_send, core_recv, own_send, own_recv, pick_send, pick_recv,
    *held,
):
    i, core, side, sibling, across, behind, ahead = neighbours(orb_count)
    s = lax.axis_index("slab")
    others = [lax.rem(s + k, slab_count) for k in range(1, slab_count)]
    rows, cells = orbital_ref.shape
    width = out_ref.shape[3] // chunks
    cols = [pl.ds(q * width, width) for q in range(chunks)]

    lane = lax.broadcasted_iota(jnp.int32, (rows, 128), 1)
    corner = jnp.zeros((rows, 128), F32)
    for c in range(3):
        corner = jnp.where(lane == c, offsets_ref[0, c].astype(F32), corner)
    out_ref[s, 0, :, pl.ds(0, cells)] = orbital_ref[...]
    out_ref[s, 0, :, pl.ds(cells, 128)] = corner.astype(BF16)
    for q in range(chunks):
        held[q][core] = out_ref[s, 0, :, cols[q]]
    greet([(p, s) for p in (sibling, across, behind, ahead)] + [(i, o) for o in others])

    z = [remote(held[q].at[core], held[q].at[2 + core], z_send.at[q], z_recv.at[q], behind, s) for q in range(chunks)]
    by_core = [
        [
            remote(held[q].at[2 * g + core], held[q].at[2 * g + core], core_send.at[g, q], core_recv.at[g, q], sibling, s)
            for q in range(chunks)
        ]
        for g in range(3)
    ]
    y_here = [remote(held[q].at[core], held[q].at[4 + core], y_send.at[q], y_recv.at[q], across, s) for q in range(chunks)]
    y_pass = [remote(held[q].at[2 + core], held[q].at[4 + core], y_send.at[q], y_recv.at[q], across, s) for q in range(chunks)]
    own = [
        remote(out_ref.at[s, 0], out_ref.at[s, 0], own_send.at[k], own_recv.at[k], i, o) for k, o in enumerate(others)
    ]
    for q in range(chunks):
        z[q].start()
    for q in range(chunks):
        pl.when(side == 1)(y_here[q].start)
    for copy in own:
        copy.start()
    for q in range(chunks):
        by_core[0][q].start()
    for q in range(chunks):
        z[q].wait_recv()
        pl.when(side == 0)(y_pass[q].start)
        by_core[1][q].start()
    slots = [slot_of(partners_ref[0, n], i, side, orb_count) for n in range(2)]
    picks = []
    for q in range(chunks):
        y_here[q].wait_recv()
        by_core[2][q].start()
        for g in range(3):
            by_core[g][q].wait_recv()
        for n in range(2):
            out_ref[s, 1 + n, :, cols[q]] = held[q][slots[n]]
            for k, o in enumerate(others):
                here = out_ref.at[s, 1 + n, :, cols[q]]
                picks.append(remote(here, here, pick_send.at[n, q, k], pick_recv.at[n, q, k], i, o))
                picks[-1].start()
    for q in range(chunks):
        z[q].wait_send()
        y_here[q].wait_send()
        for g in range(3):
            by_core[g][q].wait_send()
    for copy in own + picks:
        copy.wait()


def gather_boxes(orbitals, partners, offsets):
    orb_count, slab_count = lax.axis_size("orb"), lax.axis_size("slab")
    rows, cells = orbitals.shape[1:]
    lanes = cells + 128
    chunks = 3 if lanes % (3 * 128) == 0 else 1
    smem = pl.BlockSpec(memory_space=pltpu.SMEM)
    vmem = pl.BlockSpec(memory_space=pltpu.VMEM)
    dma = pltpu.SemaphoreType.DMA
    peers = slab_count - 1
    return pl.pallas_call(
        functools.partial(gather_kernel, orb_count, slab_count, chunks),
        out_shape=jax.ShapeDtypeStruct((slab_count, 3, rows, lanes), BF16),
        in_specs=[smem, smem, vmem],
        out_specs=vmem,
        scratch_shapes=[
            dma((chunks,)), dma((chunks,)), dma((chunks,)), dma((chunks,)),
            dma((3, chunks)), dma((3, chunks)), dma((peers,)), dma((peers,)),
            dma((2, chunks, peers)), dma((2, chunks, peers)),
        ] + [pltpu.VMEM((6, rows, lanes // chunks), BF16)] * chunks,
        compiler_params=pltpu.CompilerParams(
            collective_id=0, has_side_effects=True, vmem_limit_bytes=32 * 1024 * 1024
        ),
        name="gather_boxes",
    )(partners, offsets, orbitals.reshape(rows, cells))


def pair_kernel(
    orb_count, box_edge, k1_count,
    partners_ref, boxes_ref, kernel_ref, f2_ref, f1_ref, f0_ref, e0_ref, e1_ref, e2_ref,
    out_ref,
    cells, here, y_parts, v_parts, k_rows, terms, e1_own, e1_far, e2_own, e2_far,
    x_send, x_recv, core_send, core_recv, y_send, y_recv, z_send, z_recv,
    packed, from_slab, kept, to_core, from_core, to_y, from_y, to_z, from_z,
):
    edge = box_edge
    grid_len = 2 * edge
    half = edge // 2
    lanes = 2 * edge
    slab_count, _, rows, _ = boxes_ref.shape
    i, core, side, sibling, across, behind, ahead = neighbours(orb_count)
    slab = lax.axis_index("slab")
    others = [lax.rem(slab + k, slab_count) for k in range(1, slab_count)]
    greet([(p, slab) for p in (sibling, across, behind, ahead)] + [(i, o) for o in others])

    lane = lax.broadcasted_iota(jnp.int32, (edge, lanes), 1)
    low_lanes = lane < edge
    row = lax.broadcasted_iota(jnp.int32, (edge, lanes), 0)
    corner_lane = lax.broadcasted_iota(jnp.int32, (1, lanes), 1)

    def corner(b):
        held = boxes_ref[0, b, :, pl.ds(edge * edge, lanes)].astype(F32)[0:1]
        return [jnp.sum(jnp.where(corner_lane == c, held, 0.0)).astype(jnp.int32) for c in range(3)]

    corners = [corner(b) for b in range(3)]
    shifts = [[corners[1 + n][c] - corners[0][c] for c in range(3)] for n in range(2)]
    cell_pitch = edge + 1
    y_pitch = 2 * edge + 1
    v_pitch = 2 * k1_count + 1
    k_pitch = k1_count + 1

    e1_grid = e1_ref[slab]
    e2_grid = e2_ref[...]
    sel_lane = lax.broadcasted_iota(jnp.int32, (grid_len, lanes), 1)
    sel_row = lax.broadcasted_iota(jnp.int32, (grid_len, lanes), 0)

    def windows(d1, d2):
        pick_rows = (row + half + d1 == lane).astype(F32).astype(BF16)
        top = dot(pick_rows, e1_grid[:grid_len]).astype(BF16)
        bottom = dot(pick_rows, e1_grid[grid_len:]).astype(BF16)
        pick_cols = ((sel_lane + half + d2 == sel_row) & (sel_lane < edge)).astype(F32).astype(BF16)
        return jnp.concatenate([top, bottom], 0), dot(e2_grid, pick_cols).astype(BF16)

    e1_own[...], e2_own[...] = windows(0, 0)
    for n in range(2):
        e1_far[n], e2_far[n] = windows(shifts[n][1], shifts[n][2])

    def unpack(g, carry):
        lo_at = pl.ds(2 * g, edge, stride=cell_pitch)
        hi_at = pl.ds(2 * g + 1, edge, stride=cell_pitch)
        for b in range(3):
            both = boxes_ref[:, b, :, pl.ds(pl.multiple_of(g * lanes, lanes), lanes)].astype(F32)
            both = both.reshape(edge, lanes)
            cells[b, lo_at, :] = jnp.where(low_lanes, both, 0.0)
            cells[b, hi_at, :] = jnp.where(low_lanes, pltpu.roll(both, edge, 1), 0.0)
        for k in range(4):
            k0 = 4 * g + k
            k_rows[pl.ds(k0 * k_pitch, k1_count), :] = kernel_ref[pl.ds(pl.multiple_of(k0 * k1_count, k1_count), k1_count), :]
        return carry

    lax.fori_loop(0, edge // 2, unpack, 0, unroll=2)

    def moved(b, c0, d0, d1, d2):
        source = c0 + d0
        at = jnp.clip(source, 0, edge - 1)
        block = cells[b, pl.ds(at * cell_pitch, edge), :]
        block = pltpu.roll(block, (-d2) & (lanes - 1), 1)
        block = pltpu.roll(block, (-d1) & (edge - 1), 0)
        inside = (row + d1 >= 0) & (row + d1 < edge) & (source >= 0) & (source < edge)
        return jnp.where(inside, block, 0.0)

    batch = 4

    def forward(step, carry):
        z = []
        for j in range(batch):
            c0 = step * batch + j
            own = cells[0, pl.ds(c0 * cell_pitch, edge), :]
            for n in range(2):
                d0, d1, d2 = shifts[n]
                partner = moved(1 + n, c0, -d0, -d1, -d2)
                here[n, pl.ds(pl.multiple_of(c0 * edge, edge), edge), :] = partner
                z.append((own * partner).astype(BF16))
        z = dot(jnp.concatenate(z, 0), f2_ref[...]).astype(BF16)
        for j in range(batch):
            c0 = step * batch + j
            mine = [z[(2 * j + n) * edge : (2 * j + n + 1) * edge] for n in range(2)]
            mine = jnp.concatenate(
                [jnp.concatenate([m[:, :grid_len], m[:, grid_len:]], 0) for m in mine], 1
            )
            y = dot(f1_ref[slab], mine)
            for n in range(2):
                part = y[:, n * grid_len : (n + 1) * grid_len]
                y_parts[n, pl.ds(c0, k1_count, stride=y_pitch), :] = part[:k1_count]
                y_parts[n, pl.ds(edge + c0, k1_count, stride=y_pitch), :] = part[k1_count:]
        return carry

    lax.fori_loop(0, edge // batch, forward, 0)

    def middle(k1, carry):
        at = pl.ds(k1 * y_pitch, 2 * edge)
        y = jnp.concatenate([y_parts[n, at, :].astype(BF16) for n in range(2)], 1)
        x = dot(f0_ref[...], y)
        k = k_rows[pl.ds(k1, grid_len, stride=k_pitch), :]
        k = jnp.concatenate([k, k], 1)
        w = jnp.concatenate([(x[:grid_len] * k).astype(BF16), (x[grid_len:] * k).astype(BF16)], 0)
        v = dot(e0_ref[...], w)
        for n in range(2):
            part = v[:, n * grid_len : (n + 1) * grid_len]
            v_parts[n, pl.ds(k1, grid_len, stride=v_pitch), :] = part[:grid_len]
            v_parts[n, pl.ds(k1_count + k1, grid_len, stride=v_pitch), :] = part[grid_len:]
        return carry

    lax.fori_loop(0, k1_count, middle, 0, unroll=4)

    def v_rows(n, u0):
        u0 = jnp.clip(u0, 0, grid_len - 1)
        return v_parts[n, pl.ds(u0 * v_pitch, 2 * k1_count), :].astype(BF16)

    piece = packed.shape[2]
    pieces = rows // piece
    parts = 2
    width = edge * edge // parts
    cols = [pl.ds(h * width, width) for h in range(parts)]

    def slab_copies(number):
        to = lax.rem(slab + 1 + number // pieces, slab_count)
        return [
            remote(
                packed.at[number, :, :, cols[h]], from_slab.at[number, :, :, cols[h]],
                x_send.at[number, h], x_recv.at[number, h], i, to,
            )
            for h in range(parts)
        ]

    def one_piece(number, carry):
        target = lax.rem(slab + 1 + number // pieces, slab_count)
        first = target * rows + lax.rem(number, pieces) * piece

        def backward(step, inner):
            u = []
            for j in range(batch):
                c0 = first + step * batch + j
                v = jnp.concatenate([v_rows(n, half + c0) for n in range(2)], 1)
                part = dot(e1_own[...], v).astype(BF16)
                for n in range(2):
                    mine = part[:, n * grid_len : (n + 1) * grid_len]
                    u.append(jnp.concatenate([mine[:edge], mine[edge:]], 1))
            field = dot(jnp.concatenate(u, 0), e2_own[...])
            for j in range(batch):
                c0 = first + step * batch + j
                at = pl.ds(pl.multiple_of(c0 * edge, edge), edge)
                own = field[2 * j * edge : (2 * j + 1) * edge] * here[0, at, :]
                own += field[(2 * j + 1) * edge : (2 * j + 2) * edge] * here[1, at, :]
                terms[0, pl.ds((step * batch + j) * cell_pitch, edge), :] = own
            for n in range(2):
                d0, d1, d2 = shifts[n]
                u = []
                for j in range(batch):
                    mine = dot(e1_far[n], v_rows(n, half + d0 + first + step * batch + j)).astype(BF16)
                    u.append(jnp.concatenate([mine[:edge], mine[edge:]], 1))
                field = dot(jnp.concatenate(u, 0), e2_far[n])
                for j in range(batch):
                    there = moved(0, first + step * batch + j, d0, d1, d2)
                    to = pl.ds((step * batch + j) * cell_pitch, edge)
                    terms[1 + n, to, :] = field[j * edge : (j + 1) * edge] * there
            return inner

        lax.fori_loop(0, piece // batch, backward, 0)

        def pack(g, inner):
            for b in range(3):
                lo = terms[b, pl.ds(2 * g, piece, stride=cell_pitch), :]
                hi = terms[b, pl.ds(2 * g + 1, piece, stride=cell_pitch), :]
                both = lo + pltpu.roll(hi, edge, 1)
                packed[number, b, :, pl.ds(pl.multiple_of(g * lanes, lanes), lanes)] = both.astype(BF16)
            return inner

        lax.fori_loop(0, edge // 2, pack, 0, unroll=4)

        @pl.when(number < (slab_count - 1) * pieces)
        def _():
            for copy in slab_copies(number):
                copy.start()

        return carry

    lax.fori_loop(0, slab_count * pieces, one_piece, 0)

    slots = [slot_of(partners_ref[0, n], i, side, orb_count) for n in range(2)]
    steps = [(q, h) for q in range(pieces) for h in range(parts)]
    c = [
        remote(to_core.at[q, :, :, cols[h]], from_core.at[q, :, :, cols[h]], core_send.at[q, h], core_recv.at[q, h], sibling, slab)
        for q, h in steps
    ]
    y = [remote(to_y.at[q, :, cols[h]], from_y.at[q, :, cols[h]], y_send.at[q, h], y_recv.at[q, h], across, slab) for q, h in steps]
    z = [remote(to_z.at[q, :, cols[h]], from_z.at[q, :, cols[h]], z_send.at[q, h], z_recv.at[q, h], ahead, slab) for q, h in steps]

    def sum_slabs(t):
        q, h = steps[t]
        at = pl.ds(q * piece, piece)
        total = [packed[(slab_count - 1) * pieces + q, b, :, cols[h]].astype(F32) for b in range(3)]
        for k in range(slab_count - 1):
            slab_copies(k * pieces + q)[h].wait_recv()
            total = [total[b] + from_slab[k * pieces + q, b, :, cols[h]].astype(F32) for b in range(3)]
        out_ref[at, cols[h]] = total[0]

        def share(slot):
            return jnp.where(slots[0] == slot, total[1], jnp.where(slots[1] == slot, total[2], 0.0))

        for g in range(3):
            to_core[q, g, :, cols[h]] = share(2 * g + 1 - core).astype(BF16)
        c[t].start()
        for g in range(1, 3):
            kept[q, g - 1, :, cols[h]] = share(2 * g + core)

    def over_core(t):
        q, h = steps[t]
        at = pl.ds(q * piece, piece)
        c[t].wait_recv()
        to_y[q, :, cols[h]] = (kept[q, 1, :, cols[h]] + from_core[q, 2, :, cols[h]].astype(F32)).astype(BF16)
        y[t].start()
        out_ref[at, cols[h]] += from_core[q, 0, :, cols[h]].astype(F32)
        kept[q, 0, :, cols[h]] += from_core[q, 1, :, cols[h]].astype(F32)

    def over_y(t):
        q, h = steps[t]
        at = pl.ds(q * piece, piece)
        y[t].wait_recv()
        came = from_y[q, :, cols[h]].astype(F32)
        to_z[q, :, cols[h]] = (kept[q, 0, :, cols[h]] + jnp.where(side == 0, came, 0.0)).astype(BF16)
        z[t].start()
        out_ref[at, cols[h]] += jnp.where(side == 1, came, 0.0)

    def over_z(t):
        q, h = steps[t]
        at = pl.ds(q * piece, piece)
        z[t].wait_recv()
        out_ref[at, cols[h]] += from_z[q, :, cols[h]].astype(F32)

    stages = [sum_slabs, over_core, over_y, over_z]
    for step in range(len(steps) + len(stages) - 1):
        for position in reversed(range(len(stages))):
            if 0 <= step - position < len(steps):
                stages[position](step - position)
    for number in range((slab_count - 1) * pieces):
        for copy in slab_copies(number):
            copy.wait_send()
    for copy in c + y + z:
        copy.wait_send()


def pair_terms(boxes, partners, kernel):
    orb_count = lax.axis_size("orb")
    slab_count, _, rows, _ = boxes.shape
    box_edge = slab_count * rows
    grid_len, k1_count = kernel.shape[0], kernel.shape[1]
    tables = make_tables(box_edge, slab_count)
    smem = pl.BlockSpec(memory_space=pltpu.SMEM)
    vmem = pl.BlockSpec(memory_space=pltpu.VMEM)
    cells = box_edge * box_edge
    cell_rows = box_edge * (box_edge + 1)
    lanes = 2 * box_edge
    piece = min(rows, 16)
    pieces = rows // piece
    sent = (slab_count - 1) * pieces
    flat = (piece, cells)
    dma = pltpu.SemaphoreType.DMA
    return pl.pallas_call(
        functools.partial(pair_kernel, orb_count, box_edge, k1_count),
        out_shape=jax.ShapeDtypeStruct((rows, cells), F32),
        in_specs=[smem] + [vmem] * 8,
        out_specs=vmem,
        scratch_shapes=[
            pltpu.VMEM((3, cell_rows, lanes), F32),
            pltpu.VMEM((2, cells, lanes), F32),
            pltpu.VMEM((2, k1_count * (2 * box_edge + 1), grid_len), F32),
            pltpu.VMEM((2, grid_len * (2 * k1_count + 1), grid_len), F32),
            pltpu.VMEM((grid_len * (k1_count + 1), grid_len), F32),
            pltpu.VMEM((3, piece * (box_edge + 1), lanes), F32),
            pltpu.VMEM((2 * box_edge, 2 * k1_count), BF16),
            pltpu.VMEM((2, 2 * box_edge, 2 * k1_count), BF16),
            pltpu.VMEM((2 * grid_len, lanes), BF16),
            pltpu.VMEM((2, 2 * grid_len, lanes), BF16),
        ] + [dma((sent, 2))] * 2 + [dma((pieces, 2))] * 6 + [
            pltpu.VMEM((slab_count * pieces, 3) + flat, BF16),
            pltpu.VMEM((sent, 3) + flat, BF16),
            pltpu.VMEM((pieces, 2) + flat, F32),
            pltpu.VMEM((pieces, 3) + flat, BF16),
            pltpu.VMEM((pieces, 3) + flat, BF16),
        ] + [pltpu.VMEM((pieces,) + flat, BF16)] * 4,
        compiler_params=pltpu.CompilerParams(
            collective_id=1, has_side_effects=True, vmem_limit_bytes=60 * 1024 * 1024
        ),
        name="pair_terms",
    )(partners, boxes, kernel.reshape(grid_len * k1_count, grid_len), *tables)


def per_device(orbitals, partners, offsets, kernel):
    boxes = gather_boxes(orbitals, partners, offsets)
    return pair_terms(boxes, partners, kernel)[None]


def solution(mesh):
    return jax.shard_map(
        per_device,
        mesh=mesh,
        in_specs=(P("orb", "slab", None), P("orb", None), P("orb", None), P(None, "slab", None)),
        out_specs=P("orb", "slab", None),
        check_vma=False,
    )
```

time: 183 us -> 92.8 us (0.51)
  the two profiles are of different devices: /device:TPU:5 before, /device:TPU:0 now
where the time goes in v3:
time: 92.8 us; the launch traced here: 92.6 us
  Pallas kernels  87.3 us (94%)
  local copies, waits for them, and re-layouts  5.29 us (6%)
    pallas_call x1, Pallas kernels, pair_terms(): pl.pallas_call(functools.partial(pair_kernel, orb_count, box_edge, k1_cou...  61.5 us
    pallas_call x1, Pallas kernels, gather_boxes(): pl.pallas_call(functools.partial(gather_kernel, orb_count, slab_count, ch...  25.8 us
    unnamed x9, local copies, waits for them, and re-layouts  5.29 us

profile of v3, /device:TPU:0, one launch (start us, length us, event | category | flops | bytes accessed | tf_op | source)
XLA Modules:
  0.0 92.6 jit_solution(17045123101962476749)
XLA Ops:
  0.0 0.0 copy-start.1
  0.0 0.9 %copy-done.1 = bf16[1,32,4096]{2,1,0:T(8,128)(2,1)S(1)} copy-done((bf16[1,32,4096]{2,1,0:T(8,128)(2,1)S(1)}, bf16[1,32,4096]{2,1,0:T(8,128)(2,1)}, u32[]{:S(2)}) %copy-start.1) | copy-done | bytes 262168
  1.0 0.0 copy-start.2
  1.0 0.7 copy-done.2
  1.6 0.0 copy-start.3
  1.6 0.7 copy-done.3
  2.3 25.8 %gather_boxes.1.boxes_ref = bf16[2,3,32,4224]{3,2,1,0:T(8,128)(2,1)S(1)} custom-call(s32[1,2]{1,0:T(1,128)S(1)} %copy-done.2, s32[1,3]{1,0:T(1,128)S(1)} %copy-done.3, bf16[32,4096]{1,0:T(8,128)(2,1)S(1)} %bitcast.3), custom_call_target="tpu_custom_call" | custom-call | tf_op jit(solution)/shard_map/gather_boxes/pallas_call | solution.py:165
  28.0 0.0 copy-start
  28.0 1.2 %copy-done = bf16[2,3,32,4224]{3,2,1,0:T(8,128)(2,1)} copy-done((bf16[2,3,32,4224]{3,2,1,0:T(8,128)(2,1)}, bf16[2,3,32,4224]{3,2,1,0:T(8,128)(2,1)S(1)}, u32[]{:S(2)}) %copy-start) | copy-done | bytes 1622040
  29.2 61.5 %pair_terms.1 = f32[32,4096]{1,0:T(8,128)} custom-call(s32[1,2]{1,0:T(1,128)} %partners_ref.3, bf16[2,3,32,4224]{3,2,1,0:T(8,128)(2,1)} %copy-done, f32[8192,128]{1,0:T(8,128)} %bitcast.4, bf16[128,256]{1,0:T(8,128)(2,1)} %constant.12.clone.f2_ref, bf16[2,128,128]{2,1,0:T(8,128)(2,1)} %constant.13.clone.f1_ref, bf16[256,128]{1,0:T(8,128)(2,1)} %constant.14.clone.f0_ref, ...), custom_call_target="tpu_custom_call" | custom-call | tf_op jit(solution)/shard_map/pair_terms/pallas_call | solution.py:453
  90.7 1.9 %copy.12 = f32[1,32,4096]{2,1,0:T(8,128)} copy(f32[1,32,4096]{2,1,0:T(8,128)} %bitcast.5) | data formatting | bytes 1048576
Async XLA Ops:
  0.0 0.9 %copy-start.1 = (bf16[1,32,4096]{2,1,0:T(8,128)(2,1)S(1)}, bf16[1,32,4096]{2,1,0:T(8,128)(2,1)}, u32[]{:S(2)}) copy-start(bf16[1,32,4096]{2,1,0:T(8,128)(2,1)} %param.10) | copy-start | bytes 786436
  1.0 0.7 copy-start.2
  1.6 0.7 copy-start.3
  28.0 1.2 %copy-start = (bf16[2,3,32,4224]{3,2,1,0:T(8,128)(2,1)}, bf16[2,3,32,4224]{3,2,1,0:T(8,128)(2,1)S(1)}, u32[]{:S(2)}) copy-start(bf16[2,3,32,4224]{3,2,1,0:T(8,128)(2,1)S(1)} %gather_boxes.1.boxes_ref) | copy-start | bytes 4866052

commit v4 on v3

--- a/solution.py
+++ b/solution.py
@@ -86,12 +86,12 @@
 def gather_kernel(
     orb_count, slab_count, chunks,
     partners_ref, offsets_ref, orbital_ref, out_ref,
-    z_send, z_recv, y_send, y_recv, core_send, core_recv, own_send, own_recv, pick_send, pick_recv,
+    x_send, x_recv, z_send, z_recv, y_send, y_recv, core_send, core_recv,
     *held,
 ):
     i, core, side, sibling, across, behind, ahead = neighbours(orb_count)
     s = lax.axis_index("slab")
-    others = [lax.rem(s + k, slab_count) for k in range(1, slab_count)]
+    others = [lax.rem(s + k, slab_count) for k in range(slab_count)]
     rows, cells = orbital_ref.shape
     width = out_ref.shape[3] // chunks
     cols = [pl.ds(q * width, width) for q in range(chunks)]
@@ -104,53 +104,65 @@
     out_ref[s, 0, :, pl.ds(cells, 128)] = corner.astype(BF16)
     for q in range(chunks):
         held[q][core] = out_ref[s, 0, :, cols[q]]
-    greet([(p, s) for p in (sibling, across, behind, ahead)] + [(i, o) for o in others])
-
-    z = [remote(held[q].at[core], held[q].at[2 + core], z_send.at[q], z_recv.at[q], behind, s) for q in range(chunks)]
+    greet([(p, s) for p in (sibling, across, behind, ahead)] + [(i, o) for o in others[1:]])
+
+    units = slab_count * chunks
+
+    def along(u, source, target, send, recv, to):
+        return remote(held[u].at[source], held[u].at[target], send, recv, to, s)
+
+    x = [
+        remote(held[q].at[core], held[(slab_count - k) * chunks + q].at[core], x_send.at[k, q], x_recv.at[k, q], i, others[k])
+        for k in range(1, slab_count)
+        for q in range(chunks)
+    ]
+    x_came = [
+        remote(held[q].at[core], held[k * chunks + q].at[core], x_send.at[slab_count - k, q], x_recv.at[slab_count - k, q], i, others[k])
+        for k in range(1, slab_count)
+        for q in range(chunks)
+    ]
+    z = [along(u, core, 2 + core, z_send.at[u], z_recv.at[u], behind) for u in range(units)]
+    y_here = [along(u, core, 4 + core, y_send.at[u], y_recv.at[u], across) for u in range(units)]
+    y_pass = [along(u, 2 + core, 4 + core, y_send.at[u], y_recv.at[u], across) for u in range(units)]
     by_core = [
-        [
-            remote(held[q].at[2 * g + core], held[q].at[2 * g + core], core_send.at[g, q], core_recv.at[g, q], sibling, s)
-            for q in range(chunks)
-        ]
+        [along(u, 2 * g + core, 2 * g + core, core_send.at[g, u], core_recv.at[g, u], sibling) for u in range(units)]
         for g in range(3)
     ]
-    y_here = [remote(held[q].at[core], held[q].at[4 + core], y_send.at[q], y_recv.at[q], across, s) for q in range(chunks)]
-    y_pass = [remote(held[q].at[2 + core], held[q].at[4 + core], y_send.at[q], y_recv.at[q], across, s) for q in range(chunks)]
-    own = [
-        remote(out_ref.at[s, 0], out_ref.at[s, 0], own_send.at[k], own_recv.at[k], i, o) for k, o in enumerate(others)
-    ]
-    for q in range(chunks):
-        z[q].start()
-    for q in range(chunks):
-        pl.when(side == 1)(y_here[q].start)
-    for copy in own:
+    slots = [slot_of(partners_ref[0, n], i, side, orb_count) for n in range(2)]
+
+    def send_own(u):
+        if u >= chunks:
+            x_came[u - chunks].wait_recv()
+        z[u].start()
+        pl.when(side == 1)(y_here[u].start)
+        by_core[0][u].start()
+        if u >= chunks:
+            out_ref[others[u // chunks], 0, :, cols[u % chunks]] = held[u][core]
+
+    def pass_on(u):
+        z[u].wait_recv()
+        pl.when(side == 0)(y_pass[u].start)
+        by_core[1][u].start()
+
+    def pass_last(u):
+        y_here[u].wait_recv()
+        by_core[2][u].start()
+
+    def pick(u):
+        for g in range(3):
+            by_core[g][u].wait_recv()
+        for n in range(2):
+            out_ref[others[u // chunks], 1 + n, :, cols[u % chunks]] = held[u][slots[n]]
+
+    for copy in x:
         copy.start()
-    for q in range(chunks):
-        by_core[0][q].start()
-    for q in range(chunks):
-        z[q].wait_recv()
-        pl.when(side == 0)(y_pass[q].start)
-        by_core[1][q].start()
-    slots = [slot_of(partners_ref[0, n], i, side, orb_count) for n in range(2)]
-    picks = []
-    for q in range(chunks):
-        y_here[q].wait_recv()
-        by_core[2][q].start()
-        for g in range(3):
-            by_core[g][q].wait_recv()
-        for n in range(2):
-            out_ref[s, 1 + n, :, cols[q]] = held[q][slots[n]]
-            for k, o in enumerate(others):
-                here = out_ref.at[s, 1 + n, :, cols[q]]
-                picks.append(remote(here, here, pick_send.at[n, q, k], pick_recv.at[n, q, k], i, o))
-                picks[-1].start()
-    for q in range(chunks):
-        z[q].wait_send()
-        y_here[q].wait_send()
-        for g in range(3):
-            by_core[g][q].wait_send()
-    for copy in own + picks:
-        copy.wait()
+    stages = [(send_own, 0), (pass_on, chunks), (pass_last, chunks + 1), (pick, chunks + 2)]
+    for step in range(units + chunks + 2):
+        for stage, lag in stages:
+            if 0 <= step - lag < units:
+                stage(step - lag)
+    for copy in x + z + y_here + by_core[0] + by_core[1] + by_core[2]:
+        copy.wait_send()
 
 
 def gather_boxes(orbitals, partners, offsets):
@@ -161,17 +173,16 @@
     smem = pl.BlockSpec(memory_space=pltpu.SMEM)
     vmem = pl.BlockSpec(memory_space=pltpu.VMEM)
     dma = pltpu.SemaphoreType.DMA
-    peers = slab_count - 1
+    units = slab_count * chunks
     return pl.pallas_call(
         functools.partial(gather_kernel, orb_count, slab_count, chunks),
         out_shape=jax.ShapeDtypeStruct((slab_count, 3, rows, lanes), BF16),
         in_specs=[smem, smem, vmem],
         out_specs=vmem,
         scratch_shapes=[
-            dma((chunks,)), dma((chunks,)), dma((chunks,)), dma((chunks,)),
-            dma((3, chunks)), dma((3, chunks)), dma((peers,)), dma((peers,)),
-            dma((2, chunks, peers)), dma((2, chunks, peers)),
-        ] + [pltpu.VMEM((6, rows, lanes // chunks), BF16)] * chunks,
+            dma((slab_count, chunks)), dma((slab_count, chunks)), dma((units,)), dma((units,)), dma((units,)), dma((units,)),
+            dma((3, units)), dma((3, units)),
+        ] + [pltpu.VMEM((6, rows, lanes // chunks), BF16)] * units,
         compiler_params=pltpu.CompilerParams(
             collective_id=0, has_side_effects=True, vmem_limit_bytes=32 * 1024 * 1024
         ),
@@ -185,7 +196,7 @@
     out_ref,
     cells, here, y_parts, v_parts, k_rows, terms, e1_own, e1_far, e2_own, e2_far,
     x_send, x_recv, core_send, core_recv, y_send, y_recv, z_send, z_recv,
-    packed, from_slab, kept, to_core, from_core, to_y, from_y, to_z, from_z,
+    own_terms, kept, to_core, from_core, to_y, from_y, to_z, from_z, to_x, from_x,
 ):
     edge = box_edge
     grid_len = 2 * edge
@@ -301,23 +312,26 @@
         u0 = jnp.clip(u0, 0, grid_len - 1)
         return v_parts[n, pl.ds(u0 * v_pitch, 2 * k1_count), :].astype(BF16)
 
-    piece = packed.shape[2]
+    piece = own_terms.shape[1]
     pieces = rows // piece
-    parts = 2
-    width = edge * edge // parts
-    cols = [pl.ds(h * width, width) for h in range(parts)]
-
-    def slab_copies(number):
-        to = lax.rem(slab + 1 + number // pieces, slab_count)
-        return [
-            remote(
-                packed.at[number, :, :, cols[h]], from_slab.at[number, :, :, cols[h]],
-                x_send.at[number, h], x_recv.at[number, h], i, to,
-            )
-            for h in range(parts)
-        ]
-
-    def one_piece(number, carry):
+    numbers = slab_count * pieces
+    away = numbers - pieces
+    slots = [slot_of(partners_ref[0, n], i, side, orb_count) for n in range(2)]
+
+    def over_core(t):
+        return remote(to_core.at[t], from_core.at[t], core_send.at[t], core_recv.at[t], sibling, slab)
+
+    def over_y(t):
+        return remote(to_y.at[t], from_y.at[t], y_send.at[t], y_recv.at[t], across, slab)
+
+    def over_z(t):
+        return remote(to_z.at[t], from_z.at[t], z_send.at[t], z_recv.at[t], ahead, slab)
+
+    def over_x(t):
+        target = lax.rem(slab + 1 + t // pieces, slab_count)
+        return remote(to_x.at[t], from_x.at[t], x_send.at[t], x_recv.at[t], i, target)
+
+    def compute(number):
         target = lax.rem(slab + 1 + number // pieces, slab_count)
         first = target * rows + lax.rem(number, pieces) * piece
 
@@ -353,85 +367,68 @@
         lax.fori_loop(0, piece // batch, backward, 0)
 
         def pack(g, inner):
+            at = pl.ds(pl.multiple_of(g * lanes, lanes), lanes)
+            both = []
             for b in range(3):
                 lo = terms[b, pl.ds(2 * g, piece, stride=cell_pitch), :]
                 hi = terms[b, pl.ds(2 * g + 1, piece, stride=cell_pitch), :]
-                both = lo + pltpu.roll(hi, edge, 1)
-                packed[number, b, :, pl.ds(pl.multiple_of(g * lanes, lanes), lanes)] = both.astype(BF16)
+                both.append(lo + pltpu.roll(hi, edge, 1))
+            own_terms[number, :, at] = both[0]
+
+            def share(slot):
+                return jnp.where(slots[0] == slot, both[1], jnp.where(slots[1] == slot, both[2], 0.0))
+
+            for group in range(3):
+                to_core[number, group, :, at] = share(2 * group + 1 - core).astype(BF16)
+            for group in range(1, 3):
+                kept[number, group - 1, :, at] = share(2 * group + core)
             return inner
 
         lax.fori_loop(0, edge // 2, pack, 0, unroll=4)
-
-        @pl.when(number < (slab_count - 1) * pieces)
+        over_core(number).start()
+
+    def after_core(t):
+        over_core(t).wait_recv()
+        to_y[t] = (kept[t, 1] + from_core[t, 2].astype(F32)).astype(BF16)
+        over_y(t).start()
+        own_terms[t] += from_core[t, 0].astype(F32)
+        kept[t, 0] += from_core[t, 1].astype(F32)
+
+    def after_y(t):
+        over_y(t).wait_recv()
+        came = from_y[t].astype(F32)
+        to_z[t] = (kept[t, 0] + jnp.where(side == 0, came, 0.0)).astype(BF16)
+        over_z(t).start()
+        own_terms[t] += jnp.where(side == 1, came, 0.0)
+
+    def after_z(t):
+        over_z(t).wait_recv()
+        own_terms[t] += from_z[t].astype(F32)
+
+        @pl.when(t < away)
         def _():
-            for copy in slab_copies(number):
-                copy.start()
-
+            to_x[t] = own_terms[t].astype(BF16)
+            over_x(t).start()
+
+    def one_step(step, carry):
+        for stage, lag in ((after_core, 1), (after_y, 2), (after_z, 3), (compute, 0)):
+            pl.when((step >= lag) & (step < numbers + lag))(functools.partial(stage, step - lag))
         return carry
 
-    lax.fori_loop(0, slab_count * pieces, one_piece, 0)
-
-    slots = [slot_of(partners_ref[0, n], i, side, orb_count) for n in range(2)]
-    steps = [(q, h) for q in range(pieces) for h in range(parts)]
-    c = [
-        remote(to_core.at[q, :, :, cols[h]], from_core.at[q, :, :, cols[h]], core_send.at[q, h], core_recv.at[q, h], sibling, slab)
-        for q, h in steps
-    ]
-    y = [remote(to_y.at[q, :, cols[h]], from_y.at[q, :, cols[h]], y_send.at[q, h], y_recv.at[q, h], across, slab) for q, h in steps]
-    z = [remote(to_z.at[q, :, cols[h]], from_z.at[q, :, cols[h]], z_send.at[q, h], z_recv.at[q, h], ahead, slab) for q, h in steps]
-
-    def sum_slabs(t):
-        q, h = steps[t]
-        at = pl.ds(q * piece, piece)
-        total = [packed[(slab_count - 1) * pieces + q, b, :, cols[h]].astype(F32) for b in range(3)]
+    lax.fori_loop(0, numbers + 3, one_step, 0)
+
+    for q in range(pieces):
+        total = own_terms[away + q]
         for k in range(slab_count - 1):
-            slab_copies(k * pieces + q)[h].wait_recv()
-            total = [total[b] + from_slab[k * pieces + q, b, :, cols[h]].astype(F32) for b in range(3)]
-        out_ref[at, cols[h]] = total[0]
-
-        def share(slot):
-            return jnp.where(slots[0] == slot, total[1], jnp.where(slots[1] == slot, total[2], 0.0))
-
-        for g in range(3):
-            to_core[q, g, :, cols[h]] = share(2 * g + 1 - core).astype(BF16)
-        c[t].start()
-        for g in range(1, 3):
-            kept[q, g - 1, :, cols[h]] = share(2 * g + core)
-
-    def over_core(t):
-        q, h = steps[t]
-        at = pl.ds(q * piece, piece)
-        c[t].wait_recv()
-        to_y[q, :, cols[h]] = (kept[q, 1, :, cols[h]] + from_core[q, 2, :, cols[h]].astype(F32)).astype(BF16)
-        y[t].start()
-        out_ref[at, cols[h]] += from_core[q, 0, :, cols[h]].astype(F32)
-        kept[q, 0, :, cols[h]] += from_core[q, 1, :, cols[h]].astype(F32)
-
-    def over_y(t):
-        q, h = steps[t]
-        at = pl.ds(q * piece, piece)
-        y[t].wait_recv()
-        came = from_y[q, :, cols[h]].astype(F32)
-        to_z[q, :, cols[h]] = (kept[q, 0, :, cols[h]] + jnp.where(side == 0, came, 0.0)).astype(BF16)
-        z[t].start()
-        out_ref[at, cols[h]] += jnp.where(side == 1, came, 0.0)
-
-    def over_z(t):
-        q, h = steps[t]
-        at = pl.ds(q * piece, piece)
-        z[t].wait_recv()
-        out_ref[at, cols[h]] += from_z[q, :, cols[h]].astype(F32)
-
-    stages = [sum_slabs, over_core, over_y, over_z]
-    for step in range(len(steps) + len(stages) - 1):
-        for position in reversed(range(len(stages))):
-            if 0 <= step - position < len(steps):
-                stages[position](step - position)
-    for number in range((slab_count - 1) * pieces):
-        for copy in slab_copies(number):
-            copy.wait_send()
-    for copy in c + y + z:
-        copy.wait_send()
+            over_x(k * pieces + q).wait_recv()
+            total += from_x[k * pieces + q].astype(F32)
+        out_ref[pl.ds(q * piece, piece), :] = total
+    for t in range(numbers):
+        over_core(t).wait_send()
+        over_y(t).wait_send()
+        over_z(t).wait_send()
+        if t < away:
+            over_x(t).wait_send()
 
 
 def pair_terms(boxes, partners, kernel):
@@ -447,7 +444,8 @@
     lanes = 2 * box_edge
     piece = min(rows, 16)
     pieces = rows // piece
-    sent = (slab_count - 1) * pieces
+    numbers = slab_count * pieces
+    sent = numbers - pieces
     flat = (piece, cells)
     dma = pltpu.SemaphoreType.DMA
     return pl.pallas_call(
@@ -466,13 +464,12 @@
             pltpu.VMEM((2, 2 * box_edge, 2 * k1_count), BF16),
             pltpu.VMEM((2 * grid_len, lanes), BF16),
             pltpu.VMEM((2, 2 * grid_len, lanes), BF16),
-        ] + [dma((sent, 2))] * 2 + [dma((pieces, 2))] * 6 + [
-            pltpu.VMEM((slab_count * pieces, 3) + flat, BF16),
-            pltpu.VMEM((sent, 3) + flat, BF16),
-            pltpu.VMEM((pieces, 2) + flat, F32),
-            pltpu.VMEM((pieces, 3) + flat, BF16),
-            pltpu.VMEM((pieces, 3) + flat, BF16),
-        ] + [pltpu.VMEM((pieces,) + flat, BF16)] * 4,
+        ] + [dma((sent,))] * 2 + [dma((numbers,))] * 6 + [
+            pltpu.VMEM((numbers,) + flat, F32),
+            pltpu.VMEM((numbers, 2) + flat, F32),
+            pltpu.VMEM((numbers, 3) + flat, BF16),
+            pltpu.VMEM((numbers, 3) + flat, BF16),
+        ] + [pltpu.VMEM((numbers,) + flat, BF16)] * 4 + [pltpu.VMEM((sent,) + flat, BF16)] * 2,
         compiler_params=pltpu.CompilerParams(
             collective_id=1, has_side_effects=True, vmem_limit_bytes=60 * 1024 * 1024
         ),

time: 92.8 us -> 85.2 us (0.918)
  Pallas kernels: 87.3 us -> 79.7 us
    pallas_call x1, Pallas kernels: 61.5 us -> 57.6 us  [pair_terms(): pl.pallas_call(functools.partial(pair_kernel, orb_count, box_edge, k1_cou...]
    pallas_call x1, Pallas kernels: 25.8 us -> 22.1 us  [gather_boxes(): pl.pallas_call(functools.partial(gather_kernel, orb_count, slab_count, ch...]
where the time goes in v4:
time: 85.2 us; the launch traced here: 85 us
  Pallas kernels  79.7 us (94%)
  local copies, waits for them, and re-layouts  5.29 us (6%)
    pallas_call x1, Pallas kernels, pair_terms(): pl.pallas_call(functools.partial(pair_kernel, orb_count, box_edge, k1_cou...  57.6 us
    pallas_call x1, Pallas kernels, gather_boxes(): pl.pallas_call(functools.partial(gather_kernel, orb_count, slab_count, ch...  22.1 us
    unnamed x9, local copies, waits for them, and re-layouts  5.29 us

profile of v4, /device:TPU:0, one launch (start us, length us, event | category | flops | bytes accessed | tf_op | source)
XLA Modules:
  0.0 85.0 jit_solution(5901305622092389707)
XLA Ops:
  0.0 0.0 copy-start.1
  0.0 0.9 %copy-done.1 = bf16[1,32,4096]{2,1,0:T(8,128)(2,1)S(1)} copy-done((bf16[1,32,4096]{2,1,0:T(8,128)(2,1)S(1)}, bf16[1,32,4096]{2,1,0:T(8,128)(2,1)}, u32[]{:S(2)}) %copy-start.1) | copy-done | bytes 262168
  1.0 0.0 copy-start.2
  1.0 0.7 copy-done.2
  1.6 0.0 copy-start.3
  1.6 0.7 copy-done.3
  2.3 22.1 %gather_boxes.1.boxes_ref = bf16[2,3,32,4224]{3,2,1,0:T(8,128)(2,1)S(1)} custom-call(s32[1,2]{1,0:T(1,128)S(1)} %copy-done.2, s32[1,3]{1,0:T(1,128)S(1)} %copy-done.3, bf16[32,4096]{1,0:T(8,128)(2,1)S(1)} %bitcast.3), custom_call_target="tpu_custom_call" | custom-call | tf_op jit(solution)/shard_map/gather_boxes/pallas_call | solution.py:177
  24.4 0.0 copy-start
  24.4 1.2 %copy-done = bf16[2,3,32,4224]{3,2,1,0:T(8,128)(2,1)} copy-done((bf16[2,3,32,4224]{3,2,1,0:T(8,128)(2,1)}, bf16[2,3,32,4224]{3,2,1,0:T(8,128)(2,1)S(1)}, u32[]{:S(2)}) %copy-start) | copy-done | bytes 1622040
  25.5 57.6 %pair_terms.1 = f32[32,4096]{1,0:T(8,128)} custom-call(s32[1,2]{1,0:T(1,128)} %partners_ref.3, bf16[2,3,32,4224]{3,2,1,0:T(8,128)(2,1)} %copy-done, f32[8192,128]{1,0:T(8,128)} %bitcast.4, bf16[128,256]{1,0:T(8,128)(2,1)} %constant.12.clone.f2_ref, bf16[2,128,128]{2,1,0:T(8,128)(2,1)} %constant.13.clone.f1_ref, bf16[256,128]{1,0:T(8,128)(2,1)} %constant.14.clone.f0_ref, ...), custom_call_target="tpu_custom_call" | custom-call | tf_op jit(solution)/shard_map/pair_terms/pallas_call | solution.py:451
  83.2 1.9 %copy.12 = f32[1,32,4096]{2,1,0:T(8,128)} copy(f32[1,32,4096]{2,1,0:T(8,128)} %bitcast.5) | data formatting | bytes 1048576
Async XLA Ops:
  0.0 0.9 %copy-start.1 = (bf16[1,32,4096]{2,1,0:T(8,128)(2,1)S(1)}, bf16[1,32,4096]{2,1,0:T(8,128)(2,1)}, u32[]{:S(2)}) copy-start(bf16[1,32,4096]{2,1,0:T(8,128)(2,1)} %param.10) | copy-start | bytes 786436
  1.0 0.7 copy-start.2
  1.6 0.7 copy-start.3
  24.4 1.2 %copy-start = (bf16[2,3,32,4224]{3,2,1,0:T(8,128)(2,1)}, bf16[2,3,32,4224]{3,2,1,0:T(8,128)(2,1)S(1)}, u32[]{:S(2)}) copy-start(bf16[2,3,32,4224]{3,2,1,0:T(8,128)(2,1)S(1)} %gather_boxes.1.boxes_ref) | copy-start | bytes 4866052

commit v5 on v4

--- a/solution.py
+++ b/solution.py
@@ -192,8 +192,9 @@
 
 def pair_kernel(
     orb_count, box_edge, k1_count,
-    partners_ref, boxes_ref, kernel_ref, f2_ref, f1_ref, f0_ref, e0_ref, e1_ref, e2_ref,
+    partners_ref, boxes_ref, kernel_in, f2_in, f1_in, f0_in, e0_in, e1_in, e2_in,
     out_ref,
+    kernel_ref, f2_ref, f1_ref, f0_ref, e0_ref, e1_ref, e2_ref, in_sem,
     cells, here, y_parts, v_parts, k_rows, terms, e1_own, e1_far, e2_own, e2_far,
     x_send, x_recv, core_send, core_recv, y_send, y_recv, z_send, z_recv,
     own_terms, kept, to_core, from_core, to_y, from_y, to_z, from_z, to_x, from_x,
@@ -206,6 +207,11 @@
     i, core, side, sibling, across, behind, ahead = neighbours(orb_count)
     slab = lax.axis_index("slab")
     others = [lax.rem(slab + k, slab_count) for k in range(1, slab_count)]
+    arrays_in = [kernel_in, f2_in, f1_in, f0_in, e0_in, e1_in, e2_in]
+    arrays = [kernel_ref, f2_ref, f1_ref, f0_ref, e0_ref, e1_ref, e2_ref]
+    loads = [pltpu.make_async_copy(a, b, in_sem.at[k]) for k, (a, b) in enumerate(zip(arrays_in, arrays))]
+    for k in (6, 5, 1, 2, 0, 3, 4):
+        loads[k].start()
     greet([(p, slab) for p in (sibling, across, behind, ahead)] + [(i, o) for o in others])
 
     lane = lax.broadcasted_iota(jnp.int32, (edge, lanes), 1)
@@ -218,11 +224,48 @@
         return [jnp.sum(jnp.where(corner_lane == c, held, 0.0)).astype(jnp.int32) for c in range(3)]
 
     corners = [corner(b) for b in range(3)]
-    shifts = [[corners[1 + n][c] - corners[0][c] for c in range(3)] for n in range(2)]
-    cell_pitch = edge + 1
+    shifts = [[jnp.clip(corners[1 + n][c] - corners[0][c], -half, half) for c in range(3)] for n in range(2)]
+    cell_pitch = edge + half + 1
+    term_pitch = edge + 1
     y_pitch = 2 * edge + 1
     v_pitch = 2 * k1_count + 1
     k_pitch = k1_count + 1
+
+    no_rows = jnp.zeros((half + 8, lanes), F32)
+    for b in range(3):
+        cells[b, pl.ds(0, half), :] = jnp.zeros((half, lanes), F32)
+
+    def clear(c0, carry):
+        for b in range(3):
+            cells[b, pl.ds(c0 * cell_pitch + cell_pitch - 1, half + 8), :] = no_rows
+        return carry
+
+    lax.fori_loop(0, edge, clear, 0, unroll=4)
+    for b in range(3):
+        cells[b, pl.ds(edge * cell_pitch, edge + 2 * half), :] = jnp.zeros((edge + 2 * half, lanes), F32)
+
+    def unpack(g, carry):
+        lo_at = pl.ds(half + 2 * g, edge, stride=cell_pitch)
+        hi_at = pl.ds(half + 2 * g + 1, edge, stride=cell_pitch)
+        for b in range(3):
+            both = boxes_ref[:, b, :, pl.ds(pl.multiple_of(g * lanes, lanes), lanes)].astype(F32)
+            both = both.reshape(edge, lanes)
+            cells[b, lo_at, :] = jnp.where(low_lanes, both, 0.0)
+            cells[b, hi_at, :] = jnp.where(low_lanes, pltpu.roll(both, edge, 1), 0.0)
+        return carry
+
+    lax.fori_loop(0, edge // 2, unpack, 0, unroll=4)
+
+    for load in loads:
+        load.wait()
+
+    def spread(g, carry):
+        for k in range(4):
+            k0 = 4 * g + k
+            k_rows[pl.ds(k0 * k_pitch, k1_count), :] = kernel_ref[pl.ds(pl.multiple_of(k0 * k1_count, k1_count), k1_count), :]
+        return carry
+
+    lax.fori_loop(0, edge // 2, spread, 0, unroll=2)
 
     e1_grid = e1_ref[slab]
     e2_grid = e2_ref[...]
@@ -240,29 +283,11 @@
     for n in range(2):
         e1_far[n], e2_far[n] = windows(shifts[n][1], shifts[n][2])
 
-    def unpack(g, carry):
-        lo_at = pl.ds(2 * g, edge, stride=cell_pitch)
-        hi_at = pl.ds(2 * g + 1, edge, stride=cell_pitch)
-        for b in range(3):
-            both = boxes_ref[:, b, :, pl.ds(pl.multiple_of(g * lanes, lanes), lanes)].astype(F32)
-            both = both.reshape(edge, lanes)
-            cells[b, lo_at, :] = jnp.where(low_lanes, both, 0.0)
-            cells[b, hi_at, :] = jnp.where(low_lanes, pltpu.roll(both, edge, 1), 0.0)
-        for k in range(4):
-            k0 = 4 * g + k
-            k_rows[pl.ds(k0 * k_pitch, k1_count), :] = kernel_ref[pl.ds(pl.multiple_of(k0 * k1_count, k1_count), k1_count), :]
-        return carry
-
-    lax.fori_loop(0, edge // 2, unpack, 0, unroll=2)
-
     def moved(b, c0, d0, d1, d2):
         source = c0 + d0
-        at = jnp.clip(source, 0, edge - 1)
-        block = cells[b, pl.ds(at * cell_pitch, edge), :]
-        block = pltpu.roll(block, (-d2) & (lanes - 1), 1)
-        block = pltpu.roll(block, (-d1) & (edge - 1), 0)
-        inside = (row + d1 >= 0) & (row + d1 < edge) & (source >= 0) & (source < edge)
-        return jnp.where(inside, block, 0.0)
+        at = jnp.where((source >= 0) & (source < edge), source, edge)
+        block = cells[b, pl.ds(at * cell_pitch + half + d1, edge), :]
+        return pltpu.roll(block, (-d2) & (lanes - 1), 1)
 
     batch = 4
 
@@ -270,7 +295,7 @@
         z = []
         for j in range(batch):
             c0 = step * batch + j
-            own = cells[0, pl.ds(c0 * cell_pitch, edge), :]
+            own = cells[0, pl.ds(c0 * cell_pitch + half, edge), :]
             for n in range(2):
                 d0, d1, d2 = shifts[n]
                 partner = moved(1 + n, c0, -d0, -d1, -d2)
@@ -290,7 +315,7 @@
                 y_parts[n, pl.ds(edge + c0, k1_count, stride=y_pitch), :] = part[k1_count:]
         return carry
 
-    lax.fori_loop(0, edge // batch, forward, 0)
+    lax.fori_loop(0, edge // batch, forward, 0, unroll=2)
 
     def middle(k1, carry):
         at = pl.ds(k1 * y_pitch, 2 * edge)
@@ -306,7 +331,7 @@
             v_parts[n, pl.ds(k1_count + k1, grid_len, stride=v_pitch), :] = part[grid_len:]
         return carry
 
-    lax.fori_loop(0, k1_count, middle, 0, unroll=4)
+    lax.fori_loop(0, k1_count, middle, 0, unroll=8)
 
     def v_rows(n, u0):
         u0 = jnp.clip(u0, 0, grid_len - 1)
@@ -318,14 +343,20 @@
     away = numbers - pieces
     slots = [slot_of(partners_ref[0, n], i, side, orb_count) for n in range(2)]
 
-    def over_core(t):
-        return remote(to_core.at[t], from_core.at[t], core_send.at[t], core_recv.at[t], sibling, slab)
-
-    def over_y(t):
-        return remote(to_y.at[t], from_y.at[t], y_send.at[t], y_recv.at[t], across, slab)
-
-    def over_z(t):
-        return remote(to_z.at[t], from_z.at[t], z_send.at[t], z_recv.at[t], ahead, slab)
+    parts = 4
+    width = edge * edge // parts
+    cols = [pl.ds(h * width, width) for h in range(parts)]
+
+    def over_core(t, h):
+        return remote(
+            to_core.at[t, :, :, cols[h]], from_core.at[t, :, :, cols[h]], core_send.at[t, h], core_recv.at[t, h], sibling, slab
+        )
+
+    def over_y(t, h):
+        return remote(to_y.at[t, :, cols[h]], from_y.at[t, :, cols[h]], y_send.at[t, h], y_recv.at[t, h], across, slab)
+
+    def over_z(t, h):
+        return remote(to_z.at[t, :, cols[h]], from_z.at[t, :, cols[h]], z_send.at[t, h], z_recv.at[t, h], ahead, slab)
 
     def over_x(t):
         target = lax.rem(slab + 1 + t // pieces, slab_count)
@@ -350,7 +381,7 @@
                 at = pl.ds(pl.multiple_of(c0 * edge, edge), edge)
                 own = field[2 * j * edge : (2 * j + 1) * edge] * here[0, at, :]
                 own += field[(2 * j + 1) * edge : (2 * j + 2) * edge] * here[1, at, :]
-                terms[0, pl.ds((step * batch + j) * cell_pitch, edge), :] = own
+                terms[0, pl.ds((step * batch + j) * term_pitch, edge), :] = own
             for n in range(2):
                 d0, d1, d2 = shifts[n]
                 u = []
@@ -360,18 +391,18 @@
                 field = dot(jnp.concatenate(u, 0), e2_far[n])
                 for j in range(batch):
                     there = moved(0, first + step * batch + j, d0, d1, d2)
-                    to = pl.ds((step * batch + j) * cell_pitch, edge)
+                    to = pl.ds((step * batch + j) * term_pitch, edge)
                     terms[1 + n, to, :] = field[j * edge : (j + 1) * edge] * there
             return inner
 
-        lax.fori_loop(0, piece // batch, backward, 0)
+        lax.fori_loop(0, piece // batch, backward, 0, unroll=2)
 
         def pack(g, inner):
             at = pl.ds(pl.multiple_of(g * lanes, lanes), lanes)
             both = []
             for b in range(3):
-                lo = terms[b, pl.ds(2 * g, piece, stride=cell_pitch), :]
-                hi = terms[b, pl.ds(2 * g + 1, piece, stride=cell_pitch), :]
+                lo = terms[b, pl.ds(2 * g, piece, stride=term_pitch), :]
+                hi = terms[b, pl.ds(2 * g + 1, piece, stride=term_pitch), :]
                 both.append(lo + pltpu.roll(hi, edge, 1))
             own_terms[number, :, at] = both[0]
 
@@ -384,26 +415,33 @@
                 kept[number, group - 1, :, at] = share(2 * group + core)
             return inner
 
-        lax.fori_loop(0, edge // 2, pack, 0, unroll=4)
-        over_core(number).start()
+        for h in range(parts):
+            share_of = edge // 2 // parts
+            lax.fori_loop(h * share_of, (h + 1) * share_of, pack, 0, unroll=4)
+            over_core(number, h).start()
 
     def after_core(t):
-        over_core(t).wait_recv()
-        to_y[t] = (kept[t, 1] + from_core[t, 2].astype(F32)).astype(BF16)
-        over_y(t).start()
-        own_terms[t] += from_core[t, 0].astype(F32)
-        kept[t, 0] += from_core[t, 1].astype(F32)
+        for h in range(parts):
+            over_core(t, h).wait_recv()
+            at = cols[h]
+            to_y[t, :, at] = (kept[t, 1, :, at] + from_core[t, 2, :, at].astype(F32)).astype(BF16)
+            over_y(t, h).start()
+            own_terms[t, :, at] += from_core[t, 0, :, at].astype(F32)
+            kept[t, 0, :, at] += from_core[t, 1, :, at].astype(F32)
 
     def after_y(t):
-        over_y(t).wait_recv()
-        came = from_y[t].astype(F32)
-        to_z[t] = (kept[t, 0] + jnp.where(side == 0, came, 0.0)).astype(BF16)
-        over_z(t).start()
-        own_terms[t] += jnp.where(side == 1, came, 0.0)
+        for h in range(parts):
+            over_y(t, h).wait_recv()
+            at = cols[h]
+            came = from_y[t, :, at].astype(F32)
+            to_z[t, :, at] = (kept[t, 0, :, at] + jnp.where(side == 0, came, 0.0)).astype(BF16)
+            over_z(t, h).start()
+            own_terms[t, :, at] += jnp.where(side == 1, came, 0.0)
 
     def after_z(t):
-        over_z(t).wait_recv()
-        own_terms[t] += from_z[t].astype(F32)
+        for h in range(parts):
+            over_z(t, h).wait_recv()
+            own_terms[t, :, cols[h]] += from_z[t, :, cols[h]].astype(F32)
 
         @pl.when(t < away)
         def _():
@@ -424,9 +462,10 @@
             total += from_x[k * pieces + q].astype(F32)
         out_ref[pl.ds(q * piece, piece), :] = total
     for t in range(numbers):
-        over_core(t).wait_send()
-        over_y(t).wait_send()
-        over_z(t).wait_send()
+        for h in range(parts):
+            over_core(t, h).wait_send()
+            over_y(t, h).wait_send()
+            over_z(t, h).wait_send()
         if t < away:
             over_x(t).wait_send()
 
@@ -440,7 +479,8 @@
     smem = pl.BlockSpec(memory_space=pltpu.SMEM)
     vmem = pl.BlockSpec(memory_space=pltpu.VMEM)
     cells = box_edge * box_edge
-    cell_rows = box_edge * (box_edge + 1)
+    cell_rows = (box_edge + 1) * (box_edge + box_edge // 2 + 1) + box_edge // 2 - 1
+    arrays = [kernel.reshape(grid_len * k1_count, grid_len)] + tables
     lanes = 2 * box_edge
     piece = min(rows, 16)
     pieces = rows // piece
@@ -451,9 +491,10 @@
     return pl.pallas_call(
         functools.partial(pair_kernel, orb_count, box_edge, k1_count),
         out_shape=jax.ShapeDtypeStruct((rows, cells), F32),
-        in_specs=[smem] + [vmem] * 8,
+        in_specs=[smem, vmem] + [pl.BlockSpec(memory_space=pl.ANY)] * 7,
         out_specs=vmem,
-        scratch_shapes=[
+        scratch_shapes=[pltpu.VMEM(a.shape, a.dtype) for a in arrays] + [
+            dma((len(arrays),)),
             pltpu.VMEM((3, cell_rows, lanes), F32),
             pltpu.VMEM((2, cells, lanes), F32),
             pltpu.VMEM((2, k1_count * (2 * box_edge + 1), grid_len), F32),
@@ -464,7 +505,7 @@
             pltpu.VMEM((2, 2 * box_edge, 2 * k1_count), BF16),
             pltpu.VMEM((2 * grid_len, lanes), BF16),
             pltpu.VMEM((2, 2 * grid_len, lanes), BF16),
-        ] + [dma((sent,))] * 2 + [dma((numbers,))] * 6 + [
+        ] + [dma((sent,))] * 2 + [dma((numbers, 4))] * 6 + [
             pltpu.VMEM((numbers,) + flat, F32),
             pltpu.VMEM((numbers, 2) + flat, F32),
             pltpu.VMEM((numbers, 3) + flat, BF16),
@@ -474,7 +515,7 @@
             collective_id=1, has_side_effects=True, vmem_limit_bytes=60 * 1024 * 1024
         ),
         name="pair_terms",
-    )(partners, boxes, kernel.reshape(grid_len * k1_count, grid_len), *tables)
+    )(partners, boxes, *arrays)
 
 
 def per_device(orbitals, partners, offsets, kernel):

time: 85.2 us -> 74.1 us (0.87)
  Pallas kernels: 79.7 us -> 68.5 us
    pallas_call x1, Pallas kernels: 57.6 us -> 46.4 us  [pair_terms(): pl.pallas_call(functools.partial(pair_kernel, orb_count, box_edge, k1_cou...]
where the time goes in v5:
time: 74.1 us; the launch traced here: 73.8 us
  Pallas kernels  68.5 us (92%)
  local copies, waits for them, and re-layouts  5.29 us (7%)
    pallas_call x1, Pallas kernels, pair_terms(): pl.pallas_call(functools.partial(pair_kernel, orb_count, box_edge, k1_cou...  46.4 us
    pallas_call x1, Pallas kernels, gather_boxes(): pl.pallas_call(functools.partial(gather_kernel, orb_count, slab_count, ch...  22.1 us
    unnamed x9, local copies, waits for them, and re-layouts  5.29 us

profile of v5, /device:TPU:0, one launch (start us, length us, event | category | flops | bytes accessed | tf_op | source)
XLA Modules:
  0.0 73.8 jit_solution(13130953461170765234)
XLA Ops:
  0.0 0.0 copy-start.1
  0.0 0.9 %copy-done.1 = bf16[1,32,4096]{2,1,0:T(8,128)(2,1)S(1)} copy-done((bf16[1,32,4096]{2,1,0:T(8,128)(2,1)S(1)}, bf16[1,32,4096]{2,1,0:T(8,128)(2,1)}, u32[]{:S(2)}) %copy-start.1) | copy-done | bytes 262168
  1.0 0.0 copy-start.2
  1.0 0.7 copy-done.2
  1.6 0.0 copy-start.3
  1.6 0.7 copy-done.3
  2.3 22.1 %gather_boxes.1.boxes_ref = bf16[2,3,32,4224]{3,2,1,0:T(8,128)(2,1)S(1)} custom-call(s32[1,2]{1,0:T(1,128)S(1)} %copy-done.2, s32[1,3]{1,0:T(1,128)S(1)} %copy-done.3, bf16[32,4096]{1,0:T(8,128)(2,1)S(1)} %bitcast.3), custom_call_target="tpu_custom_call" | custom-call | tf_op jit(solution)/shard_map/gather_boxes/pallas_call | solution.py:177
  24.4 0.0 copy-start
  24.4 1.2 %copy-done = bf16[2,3,32,4224]{3,2,1,0:T(8,128)(2,1)} copy-done((bf16[2,3,32,4224]{3,2,1,0:T(8,128)(2,1)}, bf16[2,3,32,4224]{3,2,1,0:T(8,128)(2,1)S(1)}, u32[]{:S(2)}) %copy-start) | copy-done | bytes 1622040
  25.5 46.4 %pair_terms.1 = f32[32,4096]{1,0:T(8,128)} custom-call(s32[1,2]{1,0:T(1,128)} %partners_ref.3, bf16[2,3,32,4224]{3,2,1,0:T(8,128)(2,1)} %copy-done, f32[8192,128]{1,0:T(8,128)} %bitcast.4, bf16[128,256]{1,0:T(8,128)(2,1)} %constant.12.clone.f2_in, bf16[2,128,128]{2,1,0:T(8,128)(2,1)} %constant.13.clone.f1_in, bf16[256,128]{1,0:T(8,128)(2,1)} %constant.14.clone.f0_in, ...), custom_call_target="tpu_custom_call" | custom-call | tf_op jit(solution)/shard_map/pair_terms/pallas_call | solution.py:491
  72.0 1.9 %copy.12 = f32[1,32,4096]{2,1,0:T(8,128)} copy(f32[1,32,4096]{2,1,0:T(8,128)} %bitcast.5) | data formatting | bytes 1048576
Async XLA Ops:
  0.0 0.9 %copy-start.1 = (bf16[1,32,4096]{2,1,0:T(8,128)(2,1)S(1)}, bf16[1,32,4096]{2,1,0:T(8,128)(2,1)}, u32[]{:S(2)}) copy-start(bf16[1,32,4096]{2,1,0:T(8,128)(2,1)} %param.10) | copy-start | bytes 786436
  1.0 0.7 copy-start.2
  1.6 0.7 copy-start.3
  24.4 1.2 %copy-start = (bf16[2,3,32,4224]{3,2,1,0:T(8,128)(2,1)}, bf16[2,3,32,4224]{3,2,1,0:T(8,128)(2,1)S(1)}, u32[]{:S(2)}) copy-start(bf16[2,3,32,4224]{3,2,1,0:T(8,128)(2,1)S(1)} %gather_boxes.1.boxes_ref) | copy-start | bytes 4866052

commit v6 on v5

--- a/solution.py
+++ b/solution.py
@@ -23,6 +23,10 @@
 
 def block_form(cos, sin):
     return np.block([[cos, -sin], [sin, cos]])
+
+
+def halves(table):
+    return np.stack(np.split(table, 2, axis=1))
 
 
 def make_tables(box_edge, slab_count):
@@ -44,7 +48,7 @@
         e1.append(block_form(gcos[:, mine], gsin[:, mine]))
     e0 = block_form(gcos, gsin)
     e2 = np.concatenate([gcos.T, -gsin.T], 0) / grid_len**3
-    tables = [f2, np.stack(f1), f0, e0, np.stack(e1), e2]
+    tables = [halves(f2), np.stack(f1), f0, halves(e0), np.stack(e1), e2]
     return [t.astype(np.float32).astype(ml_dtypes.bfloat16) for t in tables]
 
 
@@ -83,148 +87,68 @@
     pl.semaphore_wait(barrier, len(peers))
 
 
-def gather_kernel(
-    orb_count, slab_count, chunks,
-    partners_ref, offsets_ref, orbital_ref, out_ref,
-    x_send, x_recv, z_send, z_recv, y_send, y_recv, core_send, core_recv,
-    *held,
-):
-    i, core, side, sibling, across, behind, ahead = neighbours(orb_count)
-    s = lax.axis_index("slab")
-    others = [lax.rem(s + k, slab_count) for k in range(slab_count)]
-    rows, cells = orbital_ref.shape
-    width = out_ref.shape[3] // chunks
-    cols = [pl.ds(q * width, width) for q in range(chunks)]
-
-    lane = lax.broadcasted_iota(jnp.int32, (rows, 128), 1)
-    corner = jnp.zeros((rows, 128), F32)
-    for c in range(3):
-        corner = jnp.where(lane == c, offsets_ref[0, c].astype(F32), corner)
-    out_ref[s, 0, :, pl.ds(0, cells)] = orbital_ref[...]
-    out_ref[s, 0, :, pl.ds(cells, 128)] = corner.astype(BF16)
-    for q in range(chunks):
-        held[q][core] = out_ref[s, 0, :, cols[q]]
-    greet([(p, s) for p in (sibling, across, behind, ahead)] + [(i, o) for o in others[1:]])
-
-    units = slab_count * chunks
-
-    def along(u, source, target, send, recv, to):
-        return remote(held[u].at[source], held[u].at[target], send, recv, to, s)
-
-    x = [
-        remote(held[q].at[core], held[(slab_count - k) * chunks + q].at[core], x_send.at[k, q], x_recv.at[k, q], i, others[k])
-        for k in range(1, slab_count)
-        for q in range(chunks)
-    ]
-    x_came = [
-        remote(held[q].at[core], held[k * chunks + q].at[core], x_send.at[slab_count - k, q], x_recv.at[slab_count - k, q], i, others[k])
-        for k in range(1, slab_count)
-        for q in range(chunks)
-    ]
-    z = [along(u, core, 2 + core, z_send.at[u], z_recv.at[u], behind) for u in range(units)]
-    y_here = [along(u, core, 4 + core, y_send.at[u], y_recv.at[u], across) for u in range(units)]
-    y_pass = [along(u, 2 + core, 4 + core, y_send.at[u], y_recv.at[u], across) for u in range(units)]
-    by_core = [
-        [along(u, 2 * g + core, 2 * g + core, core_send.at[g, u], core_recv.at[g, u], sibling) for u in range(units)]
-        for g in range(3)
-    ]
-    slots = [slot_of(partners_ref[0, n], i, side, orb_count) for n in range(2)]
-
-    def send_own(u):
-        if u >= chunks:
-            x_came[u - chunks].wait_recv()
-        z[u].start()
-        pl.when(side == 1)(y_here[u].start)
-        by_core[0][u].start()
-        if u >= chunks:
-            out_ref[others[u // chunks], 0, :, cols[u % chunks]] = held[u][core]
-
-    def pass_on(u):
-        z[u].wait_recv()
-        pl.when(side == 0)(y_pass[u].start)
-        by_core[1][u].start()
-
-    def pass_last(u):
-        y_here[u].wait_recv()
-        by_core[2][u].start()
-
-    def pick(u):
-        for g in range(3):
-            by_core[g][u].wait_recv()
-        for n in range(2):
-            out_ref[others[u // chunks], 1 + n, :, cols[u % chunks]] = held[u][slots[n]]
-
-    for copy in x:
-        copy.start()
-    stages = [(send_own, 0), (pass_on, chunks), (pass_last, chunks + 1), (pick, chunks + 2)]
-    for step in range(units + chunks + 2):
-        for stage, lag in stages:
-            if 0 <= step - lag < units:
-                stage(step - lag)
-    for copy in x + z + y_here + by_core[0] + by_core[1] + by_core[2]:
-        copy.wait_send()
-
-
-def gather_boxes(orbitals, partners, offsets):
-    orb_count, slab_count = lax.axis_size("orb"), lax.axis_size("slab")
-    rows, cells = orbitals.shape[1:]
-    lanes = cells + 128
-    chunks = 3 if lanes % (3 * 128) == 0 else 1
-    smem = pl.BlockSpec(memory_space=pltpu.SMEM)
-    vmem = pl.BlockSpec(memory_space=pltpu.VMEM)
-    dma = pltpu.SemaphoreType.DMA
-    units = slab_count * chunks
-    return pl.pallas_call(
-        functools.partial(gather_kernel, orb_count, slab_count, chunks),
-        out_shape=jax.ShapeDtypeStruct((slab_count, 3, rows, lanes), BF16),
-        in_specs=[smem, smem, vmem],
-        out_specs=vmem,
-        scratch_shapes=[
-            dma((slab_count, chunks)), dma((slab_count, chunks)), dma((units,)), dma((units,)), dma((units,)), dma((units,)),
-            dma((3, units)), dma((3, units)),
-        ] + [pltpu.VMEM((6, rows, lanes // chunks), BF16)] * units,
-        compiler_params=pltpu.CompilerParams(
-            collective_id=0, has_side_effects=True, vmem_limit_bytes=32 * 1024 * 1024
-        ),
-        name="gather_boxes",
-    )(partners, offsets, orbitals.reshape(rows, cells))
-
-
 def pair_kernel(
-    orb_count, box_edge, k1_count,
-    partners_ref, boxes_ref, kernel_in, f2_in, f1_in, f0_in, e0_in, e1_in, e2_in,
+    orb_count, slab_count, box_edge, k1_count, chunks,
+    partners_ref, offsets_ref, orbital_ref, kernel_in, f2_in, f1_in, f0_in, e0_in, e1_in, e2_in,
     out_ref,
-    kernel_ref, f2_ref, f1_ref, f0_ref, e0_ref, e1_ref, e2_ref, in_sem,
+    f2_ref, f1_ref, f0_ref, e0_ref, e1_ref, e2_ref, in_sem,
+    own_send, own_recv, ahead_send, ahead_recv, side_send, side_recv, sib_send, sib_recv,
     cells, here, y_parts, v_parts, k_rows, terms, e1_own, e1_far, e2_own, e2_far,
     x_send, x_recv, core_send, core_recv, y_send, y_recv, z_send, z_recv,
     own_terms, kept, to_core, from_core, to_y, from_y, to_z, from_z, to_x, from_x,
+    *held,
 ):
     edge = box_edge
     grid_len = 2 * edge
     half = edge // 2
     lanes = 2 * edge
-    slab_count, _, rows, _ = boxes_ref.shape
+    rows, cell_count = orbital_ref.shape
     i, core, side, sibling, across, behind, ahead = neighbours(orb_count)
     slab = lax.axis_index("slab")
-    others = [lax.rem(slab + k, slab_count) for k in range(1, slab_count)]
+    others = [lax.rem(slab + k, slab_count) for k in range(slab_count)]
+    kernel_ref = v_parts.at[0, pl.ds(0, grid_len * k1_count), :]
     arrays_in = [kernel_in, f2_in, f1_in, f0_in, e0_in, e1_in, e2_in]
     arrays = [kernel_ref, f2_ref, f1_ref, f0_ref, e0_ref, e1_ref, e2_ref]
     loads = [pltpu.make_async_copy(a, b, in_sem.at[k]) for k, (a, b) in enumerate(zip(arrays_in, arrays))]
     for k in (6, 5, 1, 2, 0, 3, 4):
         loads[k].start()
-    greet([(p, slab) for p in (sibling, across, behind, ahead)] + [(i, o) for o in others])
-
-    lane = lax.broadcasted_iota(jnp.int32, (edge, lanes), 1)
-    low_lanes = lane < edge
-    row = lax.broadcasted_iota(jnp.int32, (edge, lanes), 0)
-    corner_lane = lax.broadcasted_iota(jnp.int32, (1, lanes), 1)
-
-    def corner(b):
-        held = boxes_ref[0, b, :, pl.ds(edge * edge, lanes)].astype(F32)[0:1]
-        return [jnp.sum(jnp.where(corner_lane == c, held, 0.0)).astype(jnp.int32) for c in range(3)]
-
-    corners = [corner(b) for b in range(3)]
-    shifts = [[jnp.clip(corners[1 + n][c] - corners[0][c], -half, half) for c in range(3)] for n in range(2)]
+
+    per_chunk = (cell_count + lanes) // (lanes * chunks)
+    width = per_chunk * lanes
+    units = slab_count * chunks
+    corner_at = (per_chunk - 1) * lanes
+    lane = lax.broadcasted_iota(jnp.int32, (rows, lanes), 1)
+    low_half = lane < edge
+    own_corner = jnp.zeros((rows, lanes), F32)
+    for c in range(3):
+        own_corner = jnp.where(lane == c, offsets_ref[0, c].astype(F32), own_corner)
+    for q in range(chunks):
+        size = width if q < chunks - 1 else width - lanes
+        held[q][core, :, pl.ds(0, size)] = orbital_ref[:, pl.ds(q * width, size)]
+    held[chunks - 1][core, :, pl.ds(corner_at, lanes)] = own_corner.astype(BF16)
+    greet([(p, slab) for p in (sibling, across, behind, ahead)] + [(i, o) for o in others[1:]])
+
+    def along(u, source, target, send, recv, to):
+        return remote(held[u].at[source], held[u].at[target], send, recv, to, slab)
+
+    def to_slab(k, q):
+        back = slab_count - k
+        return remote(held[q].at[core], held[back * chunks + q].at[core], own_send.at[k, q], own_recv.at[k, q], i, others[k])
+
+    def from_slab(k, q):
+        back = slab_count - k
+        return remote(held[q].at[core], held[k * chunks + q].at[core], own_send.at[back, q], own_recv.at[back, q], i, others[k])
+
+    x_sends = [to_slab(k, q) for k in range(1, slab_count) for q in range(chunks)]
+    x_comes = [from_slab(k, q) for k in range(1, slab_count) for q in range(chunks)]
+    z_boxes = [along(u, core, 2 + core, ahead_send.at[u], ahead_recv.at[u], behind) for u in range(units)]
+    y_here = [along(u, core, 4 + core, side_send.at[u], side_recv.at[u], across) for u in range(units)]
+    y_pass = [along(u, 2 + core, 4 + core, side_send.at[u], side_recv.at[u], across) for u in range(units)]
+    by_core = [
+        [along(u, 2 * g + core, 2 * g + core, sib_send.at[g, u], sib_recv.at[g, u], sibling) for u in range(units)]
+        for g in range(3)
+    ]
+    slots = [slot_of(partners_ref[0, n], i, side, orb_count) for n in range(2)]
     cell_pitch = edge + half + 1
     term_pitch = edge + 1
     y_pitch = 2 * edge + 1
@@ -232,40 +156,90 @@
     k_pitch = k1_count + 1
 
     no_rows = jnp.zeros((half + 8, lanes), F32)
-    for b in range(3):
-        cells[b, pl.ds(0, half), :] = jnp.zeros((half, lanes), F32)
 
     def clear(c0, carry):
         for b in range(3):
             cells[b, pl.ds(c0 * cell_pitch + cell_pitch - 1, half + 8), :] = no_rows
         return carry
 
-    lax.fori_loop(0, edge, clear, 0, unroll=4)
-    for b in range(3):
-        cells[b, pl.ds(edge * cell_pitch, edge + 2 * half), :] = jnp.zeros((edge + 2 * half, lanes), F32)
-
-    def unpack(g, carry):
-        lo_at = pl.ds(half + 2 * g, edge, stride=cell_pitch)
-        hi_at = pl.ds(half + 2 * g + 1, edge, stride=cell_pitch)
+    def clear_all():
         for b in range(3):
-            both = boxes_ref[:, b, :, pl.ds(pl.multiple_of(g * lanes, lanes), lanes)].astype(F32)
-            both = both.reshape(edge, lanes)
-            cells[b, lo_at, :] = jnp.where(low_lanes, both, 0.0)
-            cells[b, hi_at, :] = jnp.where(low_lanes, pltpu.roll(both, edge, 1), 0.0)
-        return carry
-
-    lax.fori_loop(0, edge // 2, unpack, 0, unroll=4)
-
-    for load in loads:
-        load.wait()
+            cells[b, pl.ds(0, half), :] = jnp.zeros((half, lanes), F32)
+        lax.fori_loop(0, edge, clear, 0, unroll=4)
+        for b in range(3):
+            cells[b, pl.ds(edge * cell_pitch, edge + 2 * half), :] = jnp.zeros((edge + 2 * half, lanes), F32)
+
+    def unpack(u, b, slot):
+        k, q = u // chunks, u % chunks
+        base = others[k] * (rows * cell_pitch) + half + 2 * q * per_chunk
+
+        def one(g, carry):
+            both = held[u][slot, :, pl.ds(pl.multiple_of(g * lanes, lanes), lanes)].astype(F32)
+            cells[b, pl.ds(base + 2 * g, rows, stride=cell_pitch), :] = jnp.where(low_half, both, 0.0)
+            other = jnp.where(low_half, pltpu.roll(both, edge, 1), 0.0)
+            cells[b, pl.ds(base + 2 * g + 1, rows, stride=cell_pitch), :] = other
+            return carry
+
+        lax.fori_loop(0, per_chunk - (q == chunks - 1), one, 0, unroll=True)
 
     def spread(g, carry):
         for k in range(4):
             k0 = 4 * g + k
-            k_rows[pl.ds(k0 * k_pitch, k1_count), :] = kernel_ref[pl.ds(pl.multiple_of(k0 * k1_count, k1_count), k1_count), :]
+            at = pl.ds(pl.multiple_of(k0 * k1_count, k1_count), k1_count)
+            k_rows[pl.ds(k0 * k_pitch, k1_count), :] = v_parts[0, at, :]
         return carry
 
-    lax.fori_loop(0, edge // 2, spread, 0, unroll=2)
+    def send_own(u):
+        if u >= chunks:
+            x_comes[u - chunks].wait_recv()
+        z_boxes[u].start()
+        pl.when(side == 1)(y_here[u].start)
+        by_core[0][u].start()
+        if u >= chunks:
+            unpack(u, 0, core)
+
+    def pass_on(u):
+        z_boxes[u].wait_recv()
+        pl.when(side == 0)(y_pass[u].start)
+        by_core[1][u].start()
+
+    def pass_last(u):
+        y_here[u].wait_recv()
+        by_core[2][u].start()
+
+    def pick(u):
+        for g in range(3):
+            by_core[g][u].wait_recv()
+        for n in range(2):
+            unpack(u, 1 + n, slots[n])
+
+    for copy in x_sends:
+        copy.start()
+    stages = [(send_own, 0), (pass_on, chunks), (pass_last, chunks + 1), (pick, chunks + 2)]
+    for step in range(units + chunks + 2):
+        if step == chunks:
+            clear_all()
+            for u in range(chunks):
+                unpack(u, 0, core)
+        for stage, lag in stages:
+            if 0 <= step - lag < units:
+                stage(step - lag)
+        if step == chunks + 1:
+            for load in loads:
+                load.wait()
+            lax.fori_loop(0, edge // 2, spread, 0, unroll=2)
+
+    corner_lane = lax.broadcasted_iota(jnp.int32, (1, lanes), 1)
+
+    def corner(n):
+        came = held[chunks - 1][slots[n], :, pl.ds(corner_at, lanes)].astype(F32)[0:1]
+        return [jnp.sum(jnp.where(corner_lane == c, came, 0.0)).astype(jnp.int32) for c in range(3)]
+
+    corners = [corner(n) for n in range(2)]
+    shifts = [[jnp.clip(corners[n][c] - offsets_ref[0, c], -half, half) for c in range(3)] for n in range(2)]
+
+    row = lax.broadcasted_iota(jnp.int32, (edge, lanes), 0)
+    box_lane = lax.broadcasted_iota(jnp.int32, (edge, lanes), 1)
 
     e1_grid = e1_ref[slab]
     e2_grid = e2_ref[...]
@@ -273,7 +247,7 @@
     sel_row = lax.broadcasted_iota(jnp.int32, (grid_len, lanes), 0)
 
     def windows(d1, d2):
-        pick_rows = (row + half + d1 == lane).astype(F32).astype(BF16)
+        pick_rows = (row + half + d1 == box_lane).astype(F32).astype(BF16)
         top = dot(pick_rows, e1_grid[:grid_len]).astype(BF16)
         bottom = dot(pick_rows, e1_grid[grid_len:]).astype(BF16)
         pick_cols = ((sel_lane + half + d2 == sel_row) & (sel_lane < edge)).astype(F32).astype(BF16)
@@ -301,7 +275,7 @@
                 partner = moved(1 + n, c0, -d0, -d1, -d2)
                 here[n, pl.ds(pl.multiple_of(c0 * edge, edge), edge), :] = partner
                 z.append((own * partner).astype(BF16))
-        z = dot(jnp.concatenate(z, 0), f2_ref[...]).astype(BF16)
+        z = dot(jnp.concatenate(z, 0), jnp.concatenate([f2_ref[0], f2_ref[1]], 1)).astype(BF16)
         for j in range(batch):
             c0 = step * batch + j
             mine = [z[(2 * j + n) * edge : (2 * j + n + 1) * edge] for n in range(2)]
@@ -324,7 +298,7 @@
         k = k_rows[pl.ds(k1, grid_len, stride=k_pitch), :]
         k = jnp.concatenate([k, k], 1)
         w = jnp.concatenate([(x[:grid_len] * k).astype(BF16), (x[grid_len:] * k).astype(BF16)], 0)
-        v = dot(e0_ref[...], w)
+        v = dot(jnp.concatenate([e0_ref[0], e0_ref[1]], 1), w)
         for n in range(2):
             part = v[:, n * grid_len : (n + 1) * grid_len]
             v_parts[n, pl.ds(k1, grid_len, stride=v_pitch), :] = part[:grid_len]
@@ -341,11 +315,10 @@
     pieces = rows // piece
     numbers = slab_count * pieces
     away = numbers - pieces
-    slots = [slot_of(partners_ref[0, n], i, side, orb_count) for n in range(2)]
 
     parts = 4
-    width = edge * edge // parts
-    cols = [pl.ds(h * width, width) for h in range(parts)]
+    part_width = edge * edge // parts
+    cols = [pl.ds(h * part_width, part_width) for h in range(parts)]
 
     def over_core(t, h):
         return remote(
@@ -468,17 +441,21 @@
             over_z(t, h).wait_send()
         if t < away:
             over_x(t).wait_send()
-
-
-def pair_terms(boxes, partners, kernel):
+    for copy in x_sends + z_boxes + y_here + by_core[0] + by_core[1] + by_core[2]:
+        copy.wait_send()
+
+
+def pair_terms(orbitals, partners, offsets, kernel):
     orb_count = lax.axis_size("orb")
-    slab_count, _, rows, _ = boxes.shape
+    slab_count = lax.axis_size("slab")
+    rows, cells = orbitals.shape[1:]
     box_edge = slab_count * rows
     grid_len, k1_count = kernel.shape[0], kernel.shape[1]
     tables = make_tables(box_edge, slab_count)
     smem = pl.BlockSpec(memory_space=pltpu.SMEM)
     vmem = pl.BlockSpec(memory_space=pltpu.VMEM)
-    cells = box_edge * box_edge
+    chunks = 3 if (cells // 128 + 1) % 3 == 0 else 1
+    units = slab_count * chunks
     cell_rows = (box_edge + 1) * (box_edge + box_edge // 2 + 1) + box_edge // 2 - 1
     arrays = [kernel.reshape(grid_len * k1_count, grid_len)] + tables
     lanes = 2 * box_edge
@@ -489,12 +466,14 @@
     flat = (piece, cells)
     dma = pltpu.SemaphoreType.DMA
     return pl.pallas_call(
-        functools.partial(pair_kernel, orb_count, box_edge, k1_count),
+        functools.partial(pair_kernel, orb_count, slab_count, box_edge, k1_count, chunks),
         out_shape=jax.ShapeDtypeStruct((rows, cells), F32),
-        in_specs=[smem, vmem] + [pl.BlockSpec(memory_space=pl.ANY)] * 7,
+        in_specs=[smem, smem, vmem] + [pl.BlockSpec(memory_space=pl.ANY)] * 7,
         out_specs=vmem,
-        scratch_shapes=[pltpu.VMEM(a.shape, a.dtype) for a in arrays] + [
+        scratch_shapes=[pltpu.VMEM(a.shape, a.dtype) for a in tables] + [
             dma((len(arrays),)),
+            dma((slab_count, chunks)), dma((slab_count, chunks)), dma((units,)), dma((units,)), dma((units,)), dma((units,)),
+            dma((3, units)), dma((3, units)),
             pltpu.VMEM((3, cell_rows, lanes), F32),
             pltpu.VMEM((2, cells, lanes), F32),
             pltpu.VMEM((2, k1_count * (2 * box_edge + 1), grid_len), F32),
@@ -510,17 +489,18 @@
             pltpu.VMEM((numbers, 2) + flat, F32),
             pltpu.VMEM((numbers, 3) + flat, BF16),
             pltpu.VMEM((numbers, 3) + flat, BF16),
-        ] + [pltpu.VMEM((numbers,) + flat, BF16)] * 4 + [pltpu.VMEM((sent,) + flat, BF16)] * 2,
+        ] + [pltpu.VMEM((numbers,) + flat, BF16)] * 4 + [pltpu.VMEM((sent,) + flat, BF16)] * 2 + [
+            pltpu.VMEM((6, rows, (cells + lanes) // chunks), BF16)
+        ] * units,
         compiler_params=pltpu.CompilerParams(
-            collective_id=1, has_side_effects=True, vmem_limit_bytes=60 * 1024 * 1024
+            collective_id=0, has_side_effects=True, vmem_limit_bytes=60 * 1024 * 1024
         ),
         name="pair_terms",
-    )(partners, boxes, *arrays)
+    )(partners, offsets, orbitals.reshape(rows, cells), *arrays)
 
 
 def per_device(orbitals, partners, offsets, kernel):
-    boxes = gather_boxes(orbitals, partners, offsets)
-    return pair_terms(boxes, partners, kernel)[None]
+    return pair_terms(orbitals, partners, offsets, kernel)[None]
 
 
 def solution(mesh):

time: 74.1 us -> 66.5 us (0.90)
  Pallas kernels: 68.5 us -> 64.4 us
  local copies, waits for them, and re-layouts: 5.29 us -> 1.87 us
    pallas_call x2 -> x1, Pallas kernels: 68.5 us -> 64.4 us  [pair_terms(): pl.pallas_call(functools.partial(pair_kernel, orb_count, slab_count, box_...]
    unnamed x9 -> x1, local copies, waits for them, and re-layouts: 5.29 us -> 1.87 us
where the time goes in v6:
time: 66.5 us; the launch traced here: 66.3 us
  Pallas kernels  64.4 us (97%)
  local copies, waits for them, and re-layouts  1.87 us (3%)
    pallas_call x1, Pallas kernels, pair_terms(): pl.pallas_call(functools.partial(pair_kernel, orb_count, slab_count, box_...  64.4 us
    unnamed x1, local copies, waits for them, and re-layouts  1.87 us

profile of v6, /device:TPU:0, one launch (start us, length us, event | category | flops | bytes accessed | tf_op | source)
XLA Modules:
  0.0 66.3 jit_solution(10335297908949680308)
XLA Ops:
  0.0 64.4 %pair_terms.1 = f32[32,4096]{1,0:T(8,128)} custom-call(s32[1,2]{1,0:T(1,128)} %partners_ref.1, s32[1,3]{1,0:T(1,128)} %offsets_ref.1, bf16[32,4096]{1,0:T(8,128)(2,1)} %bitcast.5, f32[8192,128]{1,0:T(8,128)} %bitcast.3, bf16[2,128,128]{2,1,0:T(8,128)(2,1)} %constant.12.clone.f2_in, bf16[2,128,128]{2,1,0:T(8,128)(2,1)} %constant.13.clone.f1_in, ...), custom_call_target="tpu_custom_call" | custom-call | tf_op jit(solution)/shard_map/pair_terms/pallas_call | solution.py:468
  64.4 1.9 %copy.12 = f32[1,32,4096]{2,1,0:T(8,128)} copy(f32[1,32,4096]{2,1,0:T(8,128)} %bitcast.4) | data formatting | bytes 1048576

commit v7 on v6

--- a/solution.py
+++ b/solution.py
@@ -289,7 +289,7 @@
                 y_parts[n, pl.ds(edge + c0, k1_count, stride=y_pitch), :] = part[k1_count:]
         return carry
 
-    lax.fori_loop(0, edge // batch, forward, 0, unroll=2)
+    lax.fori_loop(0, edge // batch, forward, 0, unroll=4)
 
     def middle(k1, carry):
         at = pl.ds(k1 * y_pitch, 2 * edge)
@@ -335,9 +335,58 @@
         target = lax.rem(slab + 1 + t // pieces, slab_count)
         return remote(to_x.at[t], from_x.at[t], x_send.at[t], x_recv.at[t], i, target)
 
-    def compute(number):
-        target = lax.rem(slab + 1 + number // pieces, slab_count)
-        first = target * rows + lax.rem(number, pieces) * piece
+    def first_row(number):
+        return lax.rem(slab + 1 + number // pieces, slab_count) * rows + lax.rem(number, pieces) * piece
+
+    def merged(b, g):
+        lo = terms[b, pl.ds(2 * g, piece, stride=term_pitch), :]
+        hi = terms[b, pl.ds(2 * g + 1, piece, stride=term_pitch), :]
+        return lo + pltpu.roll(hi, edge, 1)
+
+    def compute_far(number):
+        first = first_row(number)
+
+        def backward(step, inner):
+            for n in range(2):
+                d0, d1, d2 = shifts[n]
+                u = []
+                for j in range(0, batch, 2):
+                    u0 = half + d0 + first + step * batch + j
+                    v = jnp.concatenate([v_rows(n, u0), v_rows(n, u0 + 1)], 1)
+                    part = dot(e1_far[n], v).astype(BF16)
+                    for c in range(2):
+                        mine = part[:, c * grid_len : (c + 1) * grid_len]
+                        u.append(jnp.concatenate([mine[:edge], mine[edge:]], 1))
+                field = dot(jnp.concatenate(u, 0), e2_far[n])
+                for j in range(batch):
+                    there = moved(0, first + step * batch + j, d0, d1, d2)
+                    to = pl.ds((step * batch + j) * term_pitch, edge)
+                    terms[1 + n, to, :] = field[j * edge : (j + 1) * edge] * there
+            return inner
+
+        lax.fori_loop(0, piece // batch, backward, 0, unroll=True)
+
+        def pack(g, inner):
+            at = pl.ds(pl.multiple_of(g * lanes, lanes), lanes)
+            both = [merged(1 + n, g) for n in range(2)]
+
+            def share(slot):
+                return jnp.where(slots[0] == slot, both[0], jnp.where(slots[1] == slot, both[1], 0.0))
+
+            for group in range(3):
+                to_core[number, group, :, at] = share(2 * group + 1 - core).astype(BF16)
+            for group in range(1, 3):
+                kept[number, group - 1, :, at] = share(2 * group + core)
+            own_terms[number, :, at] = jnp.zeros((piece, lanes), F32)
+            return inner
+
+        for h in range(parts):
+            share_of = edge // 2 // parts
+            lax.fori_loop(h * share_of, (h + 1) * share_of, pack, 0, unroll=True)
+            over_core(number, h).start()
+
+    def compute_own(number):
+        first = first_row(number)
 
         def backward(step, inner):
             u = []
@@ -355,43 +404,15 @@
                 own = field[2 * j * edge : (2 * j + 1) * edge] * here[0, at, :]
                 own += field[(2 * j + 1) * edge : (2 * j + 2) * edge] * here[1, at, :]
                 terms[0, pl.ds((step * batch + j) * term_pitch, edge), :] = own
-            for n in range(2):
-                d0, d1, d2 = shifts[n]
-                u = []
-                for j in range(batch):
-                    mine = dot(e1_far[n], v_rows(n, half + d0 + first + step * batch + j)).astype(BF16)
-                    u.append(jnp.concatenate([mine[:edge], mine[edge:]], 1))
-                field = dot(jnp.concatenate(u, 0), e2_far[n])
-                for j in range(batch):
-                    there = moved(0, first + step * batch + j, d0, d1, d2)
-                    to = pl.ds((step * batch + j) * term_pitch, edge)
-                    terms[1 + n, to, :] = field[j * edge : (j + 1) * edge] * there
             return inner
 
-        lax.fori_loop(0, piece // batch, backward, 0, unroll=2)
+        lax.fori_loop(0, piece // batch, backward, 0, unroll=True)
 
         def pack(g, inner):
-            at = pl.ds(pl.multiple_of(g * lanes, lanes), lanes)
-            both = []
-            for b in range(3):
-                lo = terms[b, pl.ds(2 * g, piece, stride=term_pitch), :]
-                hi = terms[b, pl.ds(2 * g + 1, piece, stride=term_pitch), :]
-                both.append(lo + pltpu.roll(hi, edge, 1))
-            own_terms[number, :, at] = both[0]
-
-            def share(slot):
-                return jnp.where(slots[0] == slot, both[1], jnp.where(slots[1] == slot, both[2], 0.0))
-
-            for group in range(3):
-                to_core[number, group, :, at] = share(2 * group + 1 - core).astype(BF16)
-            for group in range(1, 3):
-                kept[number, group - 1, :, at] = share(2 * group + core)
+            own_terms[number, :, pl.ds(pl.multiple_of(g * lanes, lanes), lanes)] += merged(0, g)
             return inner
 
-        for h in range(parts):
-            share_of = edge // 2 // parts
-            lax.fori_loop(h * share_of, (h + 1) * share_of, pack, 0, unroll=4)
-            over_core(number, h).start()
+        lax.fori_loop(0, edge // 2, pack, 0, unroll=8)
 
     def after_core(t):
         for h in range(parts):
@@ -422,8 +443,12 @@
             over_x(t).start()
 
     def one_step(step, carry):
-        for stage, lag in ((after_core, 1), (after_y, 2), (after_z, 3), (compute, 0)):
+        for stage, lag in ((after_core, 1), (after_y, 2), (after_z, 3), (compute_far, 0)):
             pl.when((step >= lag) & (step < numbers + lag))(functools.partial(stage, step - lag))
+        late = step >= away + 2
+        pl.when((step < away) | (late & (step < numbers + 2)))(
+            functools.partial(compute_own, jnp.where(late, step - 2, step))
+        )
         return carry
 
     lax.fori_loop(0, numbers + 3, one_step, 0)

time: 66.5 us -> 62 us (0.932)
  Pallas kernels: 64.4 us -> 59.9 us
    pallas_call x1, Pallas kernels: 64.4 us -> 59.9 us  [pair_terms(): pl.pallas_call(functools.partial(pair_kernel, orb_count, slab_count, box_...]
where the time goes in v7:
time: 62 us; the launch traced here: 61.8 us
  Pallas kernels  59.9 us (97%)
  local copies, waits for them, and re-layouts  1.87 us (3%)
    pallas_call x1, Pallas kernels, pair_terms(): pl.pallas_call(functools.partial(pair_kernel, orb_count, slab_count, box_...  59.9 us
    unnamed x1, local copies, waits for them, and re-layouts  1.87 us

profile of v7, /device:TPU:0, one launch (start us, length us, event | category | flops | bytes accessed | tf_op | source)
XLA Modules:
  0.0 61.8 jit_solution(8040621859203284304)
XLA Ops:
  0.0 59.9 %pair_terms.1 = f32[32,4096]{1,0:T(8,128)} custom-call(s32[1,2]{1,0:T(1,128)} %partners_ref.1, s32[1,3]{1,0:T(1,128)} %offsets_ref.1, bf16[32,4096]{1,0:T(8,128)(2,1)} %bitcast.5, f32[8192,128]{1,0:T(8,128)} %bitcast.3, bf16[2,128,128]{2,1,0:T(8,128)(2,1)} %constant.12.clone.f2_in, bf16[2,128,128]{2,1,0:T(8,128)(2,1)} %constant.13.clone.f1_in, ...), custom_call_target="tpu_custom_call" | custom-call | tf_op jit(solution)/shard_map/pair_terms/pallas_call | solution.py:493
  59.9 1.9 %copy.12 = f32[1,32,4096]{2,1,0:T(8,128)} copy(f32[1,32,4096]{2,1,0:T(8,128)} %bitcast.4) | data formatting | bytes 1048576

commit v8 on v7

--- a/solution.py
+++ b/solution.py
@@ -263,7 +263,7 @@
         block = cells[b, pl.ds(at * cell_pitch + half + d1, edge), :]
         return pltpu.roll(block, (-d2) & (lanes - 1), 1)
 
-    batch = 4
+    batch = 8
 
     def forward(step, carry):
         z = []
@@ -289,7 +289,7 @@
                 y_parts[n, pl.ds(edge + c0, k1_count, stride=y_pitch), :] = part[k1_count:]
         return carry
 
-    lax.fori_loop(0, edge // batch, forward, 0, unroll=4)
+    lax.fori_loop(0, edge // batch, forward, 0, unroll=2)
 
     def middle(k1, carry):
         at = pl.ds(k1 * y_pitch, 2 * edge)

time: 62 us -> 62.2 us (level)
  no operation moved by 1% of the time
where the time goes in v8:
time: 62.2 us; the launch traced here: 62 us
  Pallas kernels  60.2 us (97%)
  local copies, waits for them, and re-layouts  1.87 us (3%)
    pallas_call x1, Pallas kernels, pair_terms(): pl.pallas_call(functools.partial(pair_kernel, orb_count, slab_count, box_...  60.2 us
    unnamed x1, local copies, waits for them, and re-layouts  1.87 us

profile of v8, /device:TPU:0, one launch (start us, length us, event | category | flops | bytes accessed | tf_op | source)
XLA Modules:
  0.0 62.0 jit_solution(7187338202629474373)
XLA Ops:
  0.0 60.2 %pair_terms.1 = f32[32,4096]{1,0:T(8,128)} custom-call(s32[1,2]{1,0:T(1,128)} %partners_ref.1, s32[1,3]{1,0:T(1,128)} %offsets_ref.1, bf16[32,4096]{1,0:T(8,128)(2,1)} %bitcast.5, f32[8192,128]{1,0:T(8,128)} %bitcast.3, bf16[2,128,128]{2,1,0:T(8,128)(2,1)} %constant.12.clone.f2_in, bf16[2,128,128]{2,1,0:T(8,128)(2,1)} %constant.13.clone.f1_in, ...), custom_call_target="tpu_custom_call" | custom-call | tf_op jit(solution)/shard_map/pair_terms/pallas_call | solution.py:493
  60.2 1.9 %copy.12 = f32[1,32,4096]{2,1,0:T(8,128)} copy(f32[1,32,4096]{2,1,0:T(8,128)} %bitcast.4) | data formatting | bytes 1048576
